TPU v7x, 32 devices: a whole 2x2x4 slice. The times are simulated.
32 devices in a mesh: section: 2 (over core), seq: 16 (over z, y, x).
Axes of the slice: x: 2, y: 2, z: 4, core: 2. Of those that a mesh axis runs over, the one named last changes fastest.
Arguments:
- tokens: bfloat16 [4, 1024, 768], P(None, 'seq'), may hold values from -6 to 6
- starts: int32 [4, 1024], P(None, 'seq'), may hold values from 0 to 1, as said below
- norm_gain: float32 [2, 768], P('section'), may hold values from 0.1 to 1.9
- in_weight: bfloat16 [2, 768, 3072], P('section'), may hold values from -0.21875 to 0.21875
- conv_weight: float32 [2, 4, 1536], P('section'), may hold values from -3 to 3
- conv_bias: float32 [2, 1536], P('section'), may hold values from -3 to 3
- xproj_weight: bfloat16 [2, 1536, 80], P('section'), may hold values from -0.15625 to 0.15625
- dtproj_weight: bfloat16 [2, 48, 1536], P('section'), may hold values from -0.875 to 0.875
- dt_bias: float32 [2, 1536], P('section'), may hold values from -6 to -3
- decay_rate: float32 [2, 1536, 16], P('section'), may hold values from 0.0009765625 to 4
- skip_gain: float32 [2, 1536], P('section'), may hold values from 0.5 to 1.5
- out_weight: bfloat16 [2, 1536, 768], P('section'), may hold values from -0.4375 to 0.4375
- cotangent: bfloat16 [4, 1024, 768], P(None, 'seq'), may hold values from -6 to 6
Outputs:
- boundary: bfloat16 [2, 4, 1024, 768], P('section', None, 'seq')
- grad_norm_gain: float32 [2, 768], P('section', 'seq')
- grad_in_weight: float32 [2, 768, 3072], P('section', None, 'seq')
- grad_conv_weight: float32 [2, 4, 1536], P('section', None, 'seq')
- grad_conv_bias: float32 [2, 1536], P('section', 'seq')
- grad_xproj_weight: float32 [2, 1536, 80], P('section', 'seq')
- grad_dtproj_weight: float32 [2, 48, 1536], P('section', None, 'seq')
- grad_dt_bias: float32 [2, 1536], P('section', 'seq')
- grad_decay_rate: float32 [2, 1536, 16], P('section', 'seq')
- grad_skip_gain: float32 [2, 1536], P('section', 'seq')
- grad_out_weight: float32 [2, 1536, 768], P('section', 'seq')
Inputs may be any that keep to these rules, and one draw needn't show every extreme that they name: starts[b, t] = 1 where a packed document begins at position t of micro-batch b; in one micro-batch, drawn from the seed, it is 0 at every position, so that its single document spans the whole sequence.
All inputs are finite; a program needn't handle non-finite values.
Results may differ from a plain program's by a relative error of at most 0.035.
Values may be sent and summed in bfloat16 or wider, within the bound.
No kernel may reach another device: no remote copies, remote signals or barrier semaphores. Data moves between devices by JAX's collectives and lax.ppermute only.
A program may use at most 256 MiB of HBM per device.

v0:
```python
import jax
import jax.numpy as jnp
from jax import lax
from jax.sharding import PartitionSpec as P

EPS = 1e-05


def passed_along(array, axis, by):
    count = lax.axis_size(axis)
    pairs = [(i, i + by) for i in range(count) if 0 <= i + by < count]
    return lax.ppermute(array, axis, pairs)


def carried_in(array, axis, combine, identity):
    count, place = (lax.axis_size(axis), lax.axis_index(axis))
    everything = jax.tree.map(
        lambda part, kind: lax.all_gather(part.astype(kind), axis),
        array,
        (jnp.bfloat16, jnp.bfloat16),
    )
    start = jax.tree.map(
        lambda part, zero: jnp.broadcast_to(jnp.asarray(zero, part.dtype), part.shape),
        array,
        identity,
    )

    def carried_hop(k, before):
        reached = k < place
        new = combine(
            before, jax.tree.map(lambda part, own: part[k].astype(own.dtype), everything, array)
        )
        return jax.tree.map(lambda a, b: jnp.where(reached, a, b), new, before)

    return lax.fori_loop(0, count, carried_hop, start)


def prefix_2(array, axis, combine, identity):
    count, place = (lax.axis_size(axis), lax.axis_index(axis))
    everything = jax.tree.map(
        lambda part, kind: lax.all_gather(part.astype(kind), axis),
        array,
        jax.tree.map(lambda a: jnp.bfloat16 if a.dtype == jnp.float32 else a.dtype, array),
    )
    start = jax.tree.map(
        lambda part, zero: jnp.broadcast_to(jnp.asarray(zero, part.dtype), part.shape),
        array,
        identity,
    )

    def prefix_hop(k, before):
        at = count - 1 - k
        reached = at > place
        new = combine(
            before, jax.tree.map(lambda part, own: part[at].astype(own.dtype), everything, array)
        )
        return jax.tree.map(lambda a, b: jnp.where(reached, a, b), new, before)

    return lax.fori_loop(0, count, prefix_hop, start)


def norm_rows(source, gain_row):
    return source * lax.rsqrt(jnp.mean(source * source, axis=-1, keepdims=True) + EPS) * gain_row


def conv_mix(extended, start_ext, kernel, offset):
    free_one = 1.0 - start_ext[3:]
    free_two = free_one * (1.0 - start_ext[2:-1])
    free_three = free_two * (1.0 - start_ext[1:-2])
    summed = offset + kernel[3] * extended[3:]
    summed = summed + kernel[2] * (free_one[:, None] * extended[2:-1])
    summed = summed + kernel[1] * (free_two[:, None] * extended[1:-2])
    summed = summed + kernel[0] * (free_three[:, None] * extended[:-3])
    return jax.nn.silu(summed)


def combine(earlier, later):
    return (earlier[0] * later[0], later[0] * earlier[1] + later[1])


def gate_rows(scanned, gate_in):
    return scanned * jax.nn.silu(gate_in)


def across(left, right):
    return lax.dot_general(
        left, right, (((0,), (0,)), ((), ())), preferred_element_type=jnp.float32
    )


def against(left, right):
    return lax.dot_general(
        left, right, (((1,), (1,)), ((), ())), preferred_element_type=jnp.float32
    )


def extend(rim_part, rows_part):
    return jnp.concatenate([rim_part, rows_part], 0).astype(jnp.float32)


def rim_forward(rows_part, marks_part):
    return passed_along((rows_part, marks_part), "seq", 1)


def rim_again(rows_part, marks_part):
    return passed_along((rows_part, marks_part), "seq", 1)


def carry_forward(product, state):
    return carried_in(
        (product, state), "seq", combine, (jnp.ones_like(product), jnp.zeros_like(state))
    )


def carry_repeat(product, state):
    return carried_in(
        (product, state), "seq", combine, (jnp.ones_like(product), jnp.zeros_like(state))
    )


def carry_backward(product, state):
    return prefix_2(
        (product, state), "seq", combine, (jnp.ones_like(product), jnp.zeros_like(state))
    )


def spill_back(rows_part):
    return passed_along(rows_part, "seq", -1)


def spread_end(grads):
    return (
        lax.psum_scatter(grads[0], "seq", scatter_dimension=0, tiled=True),
        lax.psum_scatter(grads[1], "seq", scatter_dimension=1, tiled=True),
        lax.psum_scatter(grads[2], "seq", scatter_dimension=1, tiled=True),
        lax.psum_scatter(grads[3], "seq", scatter_dimension=0, tiled=True),
        lax.psum_scatter(grads[4], "seq", scatter_dimension=0, tiled=True),
        lax.psum_scatter(grads[5], "seq", scatter_dimension=1, tiled=True),
        lax.psum_scatter(grads[6], "seq", scatter_dimension=0, tiled=True),
        lax.psum_scatter(grads[7], "seq", scatter_dimension=0, tiled=True),
        lax.psum_scatter(grads[8], "seq", scatter_dimension=0, tiled=True),
        lax.psum_scatter(grads[9], "seq", scatter_dimension=0, tiled=True),
    )


def local_pieces(projected, convolved, start_rows, weights):
    weight_dt, bias_dt, rate_table = (weights[5], weights[6], weights[7])
    rank_width = weight_dt.shape[0]
    state_width = rate_table.shape[1]
    step_pre = (
        jnp.dot(projected[:, :rank_width], weight_dt, preferred_element_type=jnp.float32) + bias_dt
    )
    step_size = jax.nn.softplus(step_pre)
    kept_mask = 1.0 - start_rows.astype(jnp.float32)
    decays = kept_mask[:, None, None] * jnp.exp(-step_size[:, :, None] * rate_table[None])
    in_b = projected[:, rank_width : rank_width + state_width].astype(jnp.float32)
    drives = (step_size * convolved.astype(jnp.float32))[:, :, None] * in_b[:, None, :]
    cumulative, local_states = lax.associative_scan(combine, (decays, drives))
    return (step_pre, step_size, decays, cumulative, local_states)


def front(rows_in, start_rows, weights, send_rim, send_carry):
    gain_row, weight_in, weight_conv, bias_conv, weight_x = weights[:5]
    inner_width = weight_conv.shape[1]
    normed = norm_rows(rows_in.astype(jnp.float32), gain_row).astype(jnp.bfloat16)
    mixed = jnp.dot(normed, weight_in, preferred_element_type=jnp.float32).astype(jnp.bfloat16)
    start_marks = start_rows.astype(jnp.bfloat16)
    rim_rows, rim_marks = send_rim(mixed[-3:, :inner_width], start_marks[-3:])
    convolved = conv_mix(
        extend(rim_rows, mixed[:, :inner_width]),
        extend(rim_marks, start_marks),
        weight_conv,
        bias_conv,
    ).astype(jnp.bfloat16)
    projected = jnp.dot(convolved, weight_x, preferred_element_type=jnp.float32).astype(
        jnp.bfloat16
    )
    pieces = local_pieces(projected, convolved, start_rows, weights)
    prefix = send_carry(pieces[3][-1], pieces[4][-1])
    return ((normed, mixed, rim_rows, rim_marks, convolved, projected, prefix[1]), pieces)


def middle(kept, pieces, weights):
    mixed, convolved, projected, state_in = (kept[1], kept[4], kept[5], kept[6])
    rate_table, skip_row = (weights[7], weights[8])
    rank_width = weights[5].shape[0]
    inner_width, state_width = rate_table.shape
    states = pieces[4] + pieces[3] * state_in[None]
    out_c = projected[:, rank_width + state_width :].astype(jnp.float32)
    scanned = jnp.einsum("tdn,tn->td", states, out_c) + skip_row * convolved.astype(jnp.float32)
    gate_in = mixed[:, inner_width:].astype(jnp.float32)
    gated = gate_rows(scanned, gate_in).astype(jnp.bfloat16)
    return (states, scanned, gate_in, gated)


def backward(cotan, rows_in, start_rows, weights, kept, pieces, send_carry, send_spill):
    (
        gain_row,
        weight_in,
        weight_conv,
        bias_conv,
        weight_x,
        weight_dt,
        bias_dt,
        rate_table,
        skip_row,
        weight_out,
    ) = weights
    normed, mixed, rim_rows, rim_marks, convolved, projected, state_in = kept
    step_pre, step_size, decays, cumulative, local_states = pieces
    states, scanned, gate_in, gated = middle(kept, pieces, weights)
    rank_width = weight_dt.shape[0]
    inner_width, state_width = rate_table.shape
    row_count = rows_in.shape[0]
    conv_f32 = convolved.astype(jnp.float32)
    in_b = projected[:, rank_width : rank_width + state_width].astype(jnp.float32)
    out_c = projected[:, rank_width + state_width :].astype(jnp.float32)
    out_grad = cotan.astype(jnp.bfloat16)
    grad_out_w = across(gated, out_grad)
    gated_grad = against(out_grad, weight_out)
    scanned_grad, gate_grad = jax.vjp(gate_rows, scanned, gate_in)[1](gated_grad)
    grad_skip = jnp.sum(scanned_grad * conv_f32, 0)
    conv_grad = scanned_grad * skip_row
    out_c_grad = jnp.einsum("td,tdn->tn", scanned_grad, states)
    state_grad = scanned_grad[:, :, None] * out_c[:, None, :]
    following = jnp.concatenate([decays[1:], jnp.ones_like(decays[:1])], 0)
    reach, partial_grad = lax.associative_scan(combine, (following, state_grad), reverse=True)
    incoming = send_carry(cumulative[-1], decays[0] * partial_grad[0])[1]
    total_grad = partial_grad + reach * incoming[None]
    previous = jnp.concatenate([state_in[None], states[:-1]], 0)
    log_grad = total_grad * previous * decays
    grad_rate = -jnp.einsum("tdn,td->dn", log_grad, step_size)
    drive_grad = jnp.einsum("tdn,tn->td", total_grad, in_b)
    step_grad = -jnp.einsum("tdn,dn->td", log_grad, rate_table) + drive_grad * conv_f32
    in_b_grad = jnp.einsum("tdn,td->tn", total_grad, step_size * conv_f32)
    conv_grad = conv_grad + step_size * drive_grad
    pre_grad = step_grad * jax.nn.sigmoid(step_pre)
    grad_bias_dt = jnp.sum(pre_grad, 0)
    pre_low = pre_grad.astype(jnp.bfloat16)
    grad_dt_w = across(projected[:, :rank_width], pre_low)
    proj_grad = jnp.concatenate([against(pre_low, weight_dt), in_b_grad, out_c_grad], 1).astype(
        jnp.bfloat16
    )
    grad_x_w = across(convolved, proj_grad)
    conv_grad = conv_grad + against(proj_grad, weight_x)
    ext_rows = extend(rim_rows, mixed[:, :inner_width])
    ext_marks = extend(rim_marks, start_rows.astype(jnp.bfloat16))

    def conv_part(extended, kernel, offset):
        return conv_mix(extended, ext_marks, kernel, offset)

    ext_grad, grad_conv_w, grad_conv_b = jax.vjp(conv_part, ext_rows, weight_conv, bias_conv)[1](
        conv_grad
    )
    spill = send_spill(ext_grad[:3])
    inner_grad = ext_grad[3:] + jnp.concatenate(
        [jnp.zeros((row_count - 3, inner_width), jnp.float32), spill], 0
    )
    mixed_grad = jnp.concatenate([inner_grad, gate_grad], 1).astype(jnp.bfloat16)
    grad_in_w = across(normed, mixed_grad)
    normed_grad = against(mixed_grad, weight_in)
    input_grad, grad_gain = jax.vjp(norm_rows, rows_in.astype(jnp.float32), gain_row)[1](
        normed_grad
    )
    grads = (
        grad_gain,
        grad_in_w,
        grad_conv_w,
        grad_conv_b,
        grad_x_w,
        grad_dt_w,
        grad_bias_dt,
        grad_rate,
        grad_skip,
        grad_out_w,
    )
    return (cotan + input_grad, grads)


def put(stored, member, slot_index, is_valid):
    older = lax.dynamic_index_in_dim(stored, slot_index, 0, keepdims=False)
    return lax.dynamic_update_index_in_dim(
        stored, jnp.where(is_valid, member, older), slot_index, 0
    )


def fetch(stored, slot_index):
    return lax.dynamic_index_in_dim(stored, slot_index, 0, keepdims=False)


def local(
    tokens,
    starts,
    norm_gain,
    in_weight,
    conv_weight,
    conv_bias,
    xproj_weight,
    dtproj_weight,
    dt_bias,
    decay_rate,
    skip_gain,
    out_weight,
    cotangent,
):
    weights = (
        norm_gain[0],
        in_weight[0],
        conv_weight[0],
        conv_bias[0],
        xproj_weight[0],
        dtproj_weight[0],
        dt_bias[0],
        decay_rate[0],
        skip_gain[0],
        out_weight[0],
    )
    batch_count, row_count, model_width = tokens.shape
    section_count = lax.axis_size("section")
    section_index = lax.axis_index("section")
    step_count = batch_count + section_count - 1
    bf16 = jnp.bfloat16
    kept_init = ()

    def forward_step(step_at, state_tuple):
        received, inputs_store, outputs_store, kept_store = state_tuple
        micro_index = step_at - section_index
        is_valid = (micro_index >= 0) & (micro_index < batch_count)
        slot_index = jnp.clip(micro_index, 0, batch_count - 1)
        first_rows = fetch(tokens, jnp.clip(step_at, 0, batch_count - 1))
        rows_in = jnp.where(section_index == 0, first_rows, received)
        start_rows = fetch(starts, slot_index)
        kept, pieces = front(rows_in, start_rows, weights, rim_forward, carry_forward)
        states, scanned, gate_in, gated = middle(kept, pieces, weights)
        result = (
            rows_in.astype(jnp.float32)
            + jnp.dot(gated, weights[9], preferred_element_type=jnp.float32)
        ).astype(bf16)
        received = passed_along(result, "section", 1)
        inputs_store = put(inputs_store, rows_in, slot_index, is_valid)
        outputs_store = put(outputs_store, result, slot_index, is_valid)
        return (received, inputs_store, outputs_store, kept_store)

    blank_rows = jnp.zeros((batch_count, row_count, model_width), bf16)
    received, inputs_store, outputs_store, kept_store = lax.fori_loop(
        0,
        step_count,
        forward_step,
        (jnp.zeros((row_count, model_width), bf16), blank_rows, blank_rows, kept_init),
    )
    totals = tuple((jnp.zeros(member.shape, jnp.float32) for member in weights))

    def backward_step(step_at, state_tuple):
        received_grad, dx_store, sums_now = state_tuple
        micro_index = step_at - (section_count - 1 - section_index)
        is_valid = (micro_index >= 0) & (micro_index < batch_count)
        slot_index = jnp.clip(micro_index, 0, batch_count - 1)
        top_rows = fetch(cotangent, slot_index).astype(jnp.float32)
        cotan = jnp.where(
            section_index == section_count - 1, top_rows, received_grad.astype(jnp.float32)
        )
        rows_in = fetch(inputs_store, slot_index)
        start_rows = fetch(starts, slot_index)
        kept, pieces = front(rows_in, start_rows, weights, rim_again, carry_repeat)
        grad_rows, grads = backward(
            cotan, rows_in, start_rows, weights, kept, pieces, carry_backward, spill_back
        )
        low_rows = grad_rows.astype(bf16)
        received_grad = passed_along(low_rows, "section", -1)
        dx_store = put(dx_store, low_rows, slot_index, is_valid)
        grads = tuple((jnp.where(is_valid, member, 0.0) for member in grads))
        sums_now = tuple((total + member for total, member in zip(sums_now, grads)))
        return (received_grad, dx_store, sums_now)

    received_grad, dx_store, totals = lax.fori_loop(
        0,
        step_count,
        backward_step,
        (jnp.zeros((row_count, model_width), bf16), blank_rows, totals),
    )
    totals = spread_end(totals)
    boundary = jnp.where(section_index == 0, dx_store, outputs_store)[None]
    return (boundary,) + tuple((member[None] for member in totals))


def solution(mesh):
    in_specs = (
        P(None, "seq", None),
        P(None, "seq"),
        P("section", None),
        P("section", None, None),
        P("section", None, None),
        P("section", None),
        P("section", None, None),
        P("section", None, None),
        P("section", None),
        P("section", None, None),
        P("section", None),
        P("section", None, None),
        P(None, "seq", None),
    )
    out_specs = (
        P("section", None, "seq", None),
        P("section", "seq"),
        P("section", None, "seq"),
        P("section", None, "seq"),
        P("section", "seq"),
        P("section", "seq", None),
        P("section", None, "seq"),
        P("section", "seq"),
        P("section", "seq", None),
        P("section", "seq"),
        P("section", "seq", None),
    )
    return jax.shard_map(local, mesh=mesh, in_specs=in_specs, out_specs=out_specs, check_vma=False)
```

profile of v0, /device:TPU:0, one launch (start us, length us, event | category | flops | bytes accessed | tf_op | source)
XLA Modules:
  0.0 5969.5 jit_solution(9317376653550058682)
XLA Ops:
  9.3 1718.3 %while.157 = (s32[]{:T(128)}, bf16[64,768]{1,0:T(8,128)(2,1)S(1)}, bf16[4,64,768]{2,1,0:T(8,128)(2,1)S(1)}, bf16[4,64,768]{2,1,0:T(8,128)(2,1)}, pred[]{:T(512)}...) while((s32[]{:T(128)}, bf16[64,768]{1,0:T(8,128)(2,1)S(1)}, ...), condition=%wide.region_4.5_spmd, body=%wide.region_0.4_spmd.sunk | while | flops 515089280 | bytes 459744256 | solution.py:345
  169.4 20.0 pad.1305
  205.3 46.1 all_gather.72
  251.4 20.1 pad.1303
  287.5 39.9 all_gather.71
  514.5 20.0 pad.1305
  550.4 43.1 all_gather.72
  593.5 20.1 pad.1303
  629.6 41.3 all_gather.71
  857.1 20.0 pad.1305
  893.0 43.1 all_gather.72
  936.1 20.1 pad.1303
  972.2 41.3 all_gather.71
  1199.7 20.0 pad.1305
  1235.6 43.1 all_gather.72
  1278.7 20.1 pad.1303
  1314.8 41.3 all_gather.71
  1542.3 20.0 pad.1305
  1578.2 43.1 all_gather.72
  1621.3 20.1 pad.1303
  1657.4 41.3 all_gather.71
  1728.5 3413.6 %while.160 = (s32[]{:T(128)}, bf16[64,768]{1,0:T(8,128)(2,1)S(1)}, bf16[4,64,768]{2,1,0:T(8,128)(2,1)}, f32[768]{0:T(1024)}, f32[768,3072]{1,0:T(8,128)}, /*inde...) while((s32[]{:T(128)}, bf16[64,768]{1,0:T(8,128)(2,1)S(1)}, ...), condition=%wide.region_20.21_spmd.clone, body=%wide.region_5.20_spmd.clone.sunk | while | flops 1398485760 | bytes 1358697088 | solution.py:375
  1930.9 20.2 pad.1414
  2084.6 20.0 pad.1421
  2134.8 20.5 pad.1419
  2156.3 43.2 all_gather.73
  2199.5 43.6 all_gather.75
  2243.2 14.9 while.163
  2287.1 40.8 all_gather.74
  2612.5 20.5 pad.1414
  2766.4 20.0 pad.1421
  2816.7 20.5 pad.1419
  2838.1 43.6 all_gather.73
  2881.8 43.3 all_gather.75
  2925.0 14.8 while.163
  2968.9 41.7 all_gather.74
  3295.6 20.2 pad.1414
  3449.4 20.0 pad.1421
  3499.6 20.5 pad.1419
  3521.1 43.4 all_gather.73
  3564.5 43.3 all_gather.75
  3607.7 14.9 while.163
  3651.7 41.8 all_gather.74
  3978.3 20.5 pad.1414
  4132.3 20.0 pad.1421
  4182.5 20.5 pad.1419
  4204.0 43.6 all_gather.73
  4247.6 43.3 all_gather.75
  4290.9 14.8 while.163
  4334.8 41.7 all_gather.74
  4661.5 20.2 pad.1414
  4815.2 20.0 pad.1421
  4865.5 20.5 pad.1419
  4886.9 43.4 all_gather.73
  4930.3 43.3 all_gather.75
  4973.6 14.9 while.163
  5017.5 41.7 all_gather.74
  5161.6 74.2 %all-reduce.87 = (f32[768]{0:T(1024)S(1)}, f32[1536]{0:T(1024)S(1)}, f32[1536]{0:T(1024)S(1)}, f32[1536]{0:T(1024)S(1)}) all-reduce(f32[768]{0:T(1024)S(1)} %copy-done.158, f32[1536]{0:T(1024)S(1)} %copy-done.142, f32[1536]{0:T(1024)S(1)} %copy-done.145, f32[1536]{0:T(1024)S(1)} %copy-done.139), channel_id=2, replica_groups=mesh['section'=2,'seq'=16] {'seq'}, use_global_device_ids=true, to_apply=%region_21.22.clone | all-reduce | flops 5376 | bytes 43008
  5239.4 25.8 reduce-scatter.19.cloned.1.call-done
  5266.6 124.8 %reduce-scatter.25.cloned.1.call-done = f32[96,16]{1,0:T(8,128)} async-done(((f32[1536,16]{1,0:T(8,128)}), f32[96,16]{1,0:T(8,128)}) %reduce-scatter.25.cloned.1.call-update) | async-done | bytes 6160
  5392.9 124.8 %reduce-scatter.23.cloned.1.call-done = f32[96,48]{1,0:T(8,128)} async-done(((f32[1536,48]{1,0:T(8,128)}), f32[96,48]{1,0:T(8,128)}) %reduce-scatter.23.cloned.1.call-update) | async-done | bytes 18448
  5519.2 124.6 %reduce-scatter.21.cloned.1.call-done = f32[96,80]{1,0:T(8,128)} async-done(((f32[1536,80]{1,0:T(8,128)}), f32[96,80]{1,0:T(8,128)}) %reduce-scatter.21.cloned.1.call-update) | async-done | bytes 30736
  5645.2 140.2 %reduce-scatter.17.cloned.1.call-done = f32[96,768]{1,0:T(8,128)} async-done(((f32[1536,768]{1,0:T(8,128)}), f32[96,768]{1,0:T(8,128)}) %reduce-scatter.17.cloned.1.call-update) | async-done | bytes 294928 | tf_op jit(solution)/shard_map/reduce_scatter | solution.py:142
  5785.4 177.0 %reduce-scatter.15.cloned.1.call-done = f32[768,192]{0,1:T(8,128)} async-done(((f32[768,3072]{0,1:T(8,128)}), f32[768,192]{0,1:T(8,128)}) %reduce-scatter.15.cloned.1.call-update) | async-done | bytes 589840 | tf_op jit(solution)/shard_map/reduce_scatter | solution.py:134
  (3591 shorter events, 3712.3 us)
Async XLA Ops:
  7.2 5258.0 %reduce-scatter.19.cloned.1.call-start = ((), (), s32[]{:S(2)}) async-start(), calls=%async_computation.8 | async-start | bytes 835584
  14.8 11.0 collective-permute-start.4
  19.9 5.8 collective-permute-start.5
  354.3 2.2 collective-permute-start.6
  361.9 9.0 collective-permute-start.4
  366.4 4.3 collective-permute-start.5
  697.7 2.2 collective-permute-start.6
  705.3 8.1 collective-permute-start.4
  709.0 4.3 collective-permute-start.5
  1040.2 2.2 collective-permute-start.6
  1047.9 8.2 collective-permute-start.4
  1051.6 4.3 collective-permute-start.5
  1382.9 2.2 collective-permute-start.6
  1390.5 8.2 collective-permute-start.4
  1394.2 4.3 collective-permute-start.5
  1725.5 2.2 collective-permute-start.6
  1733.6 8.1 collective-permute-start
  1737.1 4.4 collective-permute-start.1
  1930.9 29.6 slice-start.2
  2134.8 64.7 %copy-start.116 = (bf16[1,1536,16]{1,2,0:T(8,128)(2,1)S(1)}, bf16[1,1536,16]{1,2,0:T(8,128)(2,1)}, u32[]{:S(2)}) copy-start(bf16[1,1536,16]{1,2,0:T(8,128)(2,1)} %get-tuple-element.2480) | copy-start | bytes 147460 | tf_op jit(solution)/shard_map/while
  2134.8 123.2 %copy-start.30 = (f32[32,1536,16]{1,2,0:T(8,128)S(1)}, f32[32,1536,16]{1,2,0:T(8,128)}, u32[]{:S(2)}) copy-start(f32[32,1536,16]{1,2,0:T(8,128)} %add.2080) | copy-start | bytes 9437188 | tf_op jit(solution)/shard_map/while
  2273.1 54.9 copy-start.45
  2327.9 27.4 slice-start.16
  2390.9 7.2 collective-permute-start.2
  2403.8 3.2 collective-permute-start.3
  2412.1 11.5 collective-permute-start
  2416.7 6.7 collective-permute-start.1
  2612.5 29.8 slice-start.2
  2816.7 65.1 %copy-start.116 = (bf16[1,1536,16]{1,2,0:T(8,128)(2,1)S(1)}, bf16[1,1536,16]{1,2,0:T(8,128)(2,1)}, u32[]{:S(2)}) copy-start(bf16[1,1536,16]{1,2,0:T(8,128)(2,1)} %get-tuple-element.2480) | copy-start | bytes 147460 | tf_op jit(solution)/shard_map/while
  2816.7 123.2 %copy-start.30 = (f32[32,1536,16]{1,2,0:T(8,128)S(1)}, f32[32,1536,16]{1,2,0:T(8,128)}, u32[]{:S(2)}) copy-start(f32[32,1536,16]{1,2,0:T(8,128)} %add.2080) | copy-start | bytes 9437188 | tf_op jit(solution)/shard_map/while
  2954.9 55.7 copy-start.45
  3010.6 27.4 slice-start.16
  3073.6 8.5 collective-permute-start.2
  3087.8 3.2 collective-permute-start.3
  3096.1 10.4 collective-permute-start
  3100.8 5.6 collective-permute-start.1
  3295.6 29.6 slice-start.2
  3499.6 64.9 %copy-start.116 = (bf16[1,1536,16]{1,2,0:T(8,128)(2,1)S(1)}, bf16[1,1536,16]{1,2,0:T(8,128)(2,1)}, u32[]{:S(2)}) copy-start(bf16[1,1536,16]{1,2,0:T(8,128)(2,1)} %get-tuple-element.2480) | copy-start | bytes 147460 | tf_op jit(solution)/shard_map/while
  3499.6 123.0 %copy-start.30 = (f32[32,1536,16]{1,2,0:T(8,128)S(1)}, f32[32,1536,16]{1,2,0:T(8,128)}, u32[]{:S(2)}) copy-start(f32[32,1536,16]{1,2,0:T(8,128)} %add.2080) | copy-start | bytes 9437188 | tf_op jit(solution)/shard_map/while
  3637.6 55.8 copy-start.45
  3756.4 8.7 collective-permute-start.2
  3770.7 3.2 collective-permute-start.3
  3779.0 10.4 collective-permute-start
  3783.7 5.6 collective-permute-start.1
  3978.3 29.8 slice-start.2
  4182.5 65.1 %copy-start.116 = (bf16[1,1536,16]{1,2,0:T(8,128)(2,1)S(1)}, bf16[1,1536,16]{1,2,0:T(8,128)(2,1)}, u32[]{:S(2)}) copy-start(bf16[1,1536,16]{1,2,0:T(8,128)(2,1)} %get-tuple-element.2480) | copy-start | bytes 147460 | tf_op jit(solution)/shard_map/while
  4182.5 123.2 %copy-start.30 = (f32[32,1536,16]{1,2,0:T(8,128)S(1)}, f32[32,1536,16]{1,2,0:T(8,128)}, u32[]{:S(2)}) copy-start(f32[32,1536,16]{1,2,0:T(8,128)} %add.2080) | copy-start | bytes 9437188 | tf_op jit(solution)/shard_map/while
  4320.7 55.8 copy-start.45
  4439.5 8.5 collective-permute-start.2
  4453.6 3.2 collective-permute-start.3
  4462.0 10.4 collective-permute-start
  4466.6 5.6 collective-permute-start.1
  4661.5 29.6 slice-start.2
  4865.5 64.9 %copy-start.116 = (bf16[1,1536,16]{1,2,0:T(8,128)(2,1)S(1)}, bf16[1,1536,16]{1,2,0:T(8,128)(2,1)}, u32[]{:S(2)}) copy-start(bf16[1,1536,16]{1,2,0:T(8,128)(2,1)} %get-tuple-element.2480) | copy-start | bytes 147460 | tf_op jit(solution)/shard_map/while
  4865.5 123.0 %copy-start.30 = (f32[32,1536,16]{1,2,0:T(8,128)S(1)}, f32[32,1536,16]{1,2,0:T(8,128)}, u32[]{:S(2)}) copy-start(f32[32,1536,16]{1,2,0:T(8,128)} %add.2080) | copy-start | bytes 9437188 | tf_op jit(solution)/shard_map/while
  5003.5 55.7 copy-start.45
  5059.2 27.4 slice-start.16
  5122.2 8.7 collective-permute-start.2
  5136.5 3.2 collective-permute-start.3
  5144.1 247.3 %reduce-scatter.25.cloned.1.call-start = ((), (), s32[]{:S(2)}) async-start(), calls=%async_computation.11 | async-start | bytes 835584
  5146.3 371.4 %reduce-scatter.23.cloned.1.call-start = ((), (), s32[]{:S(2)}) async-start(), calls=%async_computation.10 | async-start | bytes 835584
  5147.5 496.2 %reduce-scatter.21.cloned.1.call-start = ((), (), s32[]{:S(2)}) async-start(), calls=%async_computation.9 | async-start | bytes 835584
  5148.8 636.6 %reduce-scatter.17.cloned.1.call-start = ((), (), s32[]{:S(2)}) async-start(), calls=%async_computation.7 | async-start | bytes 5013504 | tf_op jit(solution)/shard_map/reduce_scatter | solution.py:142
  5149.4 813.1 %reduce-scatter.15.cloned.1.call-start = ((), (), s32[]{:S(2)}) async-start(), calls=%async_computation.6 | async-start | bytes 10027008 | tf_op jit(solution)/shard_map/reduce_scatter | solution.py:134
  (899 other events, 5524.0 us)
Sparse Core Ops, SparseCore 0:
  5144.3 120.8 reduce-scatter.18
  5269.9 121.4 reduce-scatter.24
  5396.1 121.5 reduce-scatter.22
  5522.2 121.4 reduce-scatter.20
  5649.3 136.0 reduce-scatter.16
  5792.5 169.9 reduce-scatter.14
where the time goes:
time: 6050 us; the launch traced here: 5970 us
  local copies, waits for them, and re-layouts  2440 us (40%)
  other arithmetic  1320 us (22%)
  blocking collectives  1140 us (19%)
  waiting for transfers between devices  732 us (12%)
  matrix products  212 us (4%)
  starting transfers between devices  90.6 us (1%)
    pad x200, local copies, waits for them, and re-layouts, local_pieces(): cumulative, local_states = lax.associative_scan(combine, (decays, drives))  1370 us
    pad x100, local copies, waits for them, and re-layouts, backward(): lax.associative_scan(combine, (following, state_grad), reverse=True)  777 us
    all_gather x15, blocking collectives, carried_in(): lax.all_gather(part.astype(kind), axis)  631 us
    all_gather x10, blocking collectives, prefix_2(): lax.all_gather(part.astype(kind), axis)  434 us
    unnamed x10, waiting for transfers between devices  401 us
    mul x90, other arithmetic, combine(): return (earlier[0] * later[0], later[0] * earlier[1] + later[1])  237 us
    add x60, other arithmetic, backward(): lax.associative_scan(combine, (following, state_grad), reverse=True)  192 us
    add x100, other arithmetic, local_pieces(): cumulative, local_states = lax.associative_scan(combine, (decays, drives))  185 us
  transfers between devices with their start and end apart: 41, of which 16 were waited for; matrix products, arithmetic and copies ran while one was open for 1% of the time, Pallas kernels for 0%

commit v1 on v0

v1 whole, which is shorter than its diff:
```python
import functools
import jax
import jax.numpy as jnp
from jax import lax
from jax.experimental import pallas as pl
from jax.experimental.pallas import tpu as pltpu
from jax.sharding import PartitionSpec as P

EPS = 1e-05
LOG2E = 1.4426950408889634
STOP = 1e7
LANES = 128
BLOCK = 256
TILES = BLOCK // LANES
F32 = jnp.float32
BF16 = jnp.bfloat16
VMEM_LIMIT = 56 * 1024 * 1024


def dot(left, right):
    return jnp.dot(left, right, preferred_element_type=F32)


def across(left, right):
    return lax.dot_general(left, right, (((0,), (0,)), ((), ())), preferred_element_type=F32)


def against(left, right):
    return lax.dot_general(left, right, (((1,), (1,)), ((), ())), preferred_element_type=F32)


def norm_rows(source, gain_row):
    return source * lax.rsqrt(jnp.mean(source * source, axis=-1, keepdims=True) + EPS) * gain_row


def softplus(v):
    return jnp.maximum(v, 0.0) + jnp.log1p(jnp.exp(-jnp.abs(v)))


def silu_slope(v):
    gate = jax.nn.sigmoid(v)
    return gate * (1.0 + v * (1.0 - gate))


def pair_up(left, right, row_ids, width):
    mask = (row_ids % (2 * width)) < width
    kept = jnp.where(mask, left, right)
    moved = jnp.where(mask, right, left)
    return kept + pltpu.roll(moved, 8 - width, 0)


def fold_rows(parts, row_ids):
    width = 1
    while len(parts) > 1:
        parts = [
            pair_up(parts[i], parts[i + 1], row_ids, width) for i in range(0, len(parts), 2)
        ]
        width *= 2
    return parts[0]


def halves(v):
    return v[:8] + v[8:]


def spread_columns(table, first, target):
    width = target.shape[1]
    for t in range(target.shape[0]):
        column = table[first : first + width, t : t + 1]
        target[t] = jnp.broadcast_to(column, (width, LANES))


def block_at(i):
    return pl.ds(pl.multiple_of(i * BLOCK, BLOCK), BLOCK)


def tile_at(i, lt):
    return pl.ds(pl.multiple_of(i * BLOCK + lt * LANES, LANES), LANES)


def local_scan(batches, span, blocks, seff, x, bx, at, final):
    def over_block(i, carry):
        rate = [at[:, tile_at(i, lt)] for lt in range(TILES)]

        def chunk(tc, states):
            states = list(states)
            for b in range(batches):
                rows = pl.ds(pl.multiple_of(b * span + tc * 8, 8), 8)
                for lt in range(TILES):
                    s8 = seff[rows, tile_at(i, lt)]
                    x8 = x[rows, tile_at(i, lt)]
                    h = states[b * TILES + lt]
                    for j in range(8):
                        decay = jnp.exp2(s8[j : j + 1] * rate[lt])
                        h = decay * h + x8[j : j + 1] * bx[b * span + tc * 8 + j]
                    states[b * TILES + lt] = h
            return tuple(states)

        zero = jnp.zeros((at.shape[0], LANES), F32)
        states = lax.fori_loop(0, span // 8, chunk, (zero,) * (batches * TILES))
        for b in range(batches):
            for lt in range(TILES):
                final[b, :, tile_at(i, lt)] = states[b * TILES + lt]
        return carry

    lax.fori_loop(0, blocks, over_block, 0)


def front_kernel(
    batches, span, width, rank, states_n,
    mixed, rim, marks, cw, cb, xw, dw, db, at,
    pre_o, conv_o, proj_o, spre_o, bx_o, cx_o, final_o, total_o,
    ext, seff, x,
):
    m = marks[...]
    for b in range(batches):
        lo, hi = b * span, (b + 1) * span
        ext[b, 0:8] = rim[b]
        ext[b, 8:] = mixed[lo:hi, :width].astype(F32)
        v = cb[...] + cw[3:4] * ext[b, 8 : 8 + span]
        for k in (1, 2, 3):
            v = v + cw[3 - k : 4 - k] * (m[lo:hi, k : k + 1] * ext[b, 8 - k : 8 - k + span])
        pre_o[lo:hi] = v
    conv = jax.nn.silu(pre_o[...]).astype(BF16)
    conv_o[...] = conv
    proj = dot(conv, xw[...])
    proj_o[...] = proj.astype(BF16)
    spre = dot(proj_o[...], dw[...]) + db[...]
    spre_o[...] = spre
    step = softplus(spre)
    seff[...] = step + m[:, 0:1] * STOP
    x[...] = step * conv.astype(F32)
    for b in range(batches):
        total_o[b] = jnp.sum(seff[b * span : (b + 1) * span], axis=0, keepdims=True)
    table = proj.astype(BF16).astype(F32).T
    spread_columns(table, rank, bx_o)
    spread_columns(table, rank + states_n, cx_o)
    local_scan(batches, span, width // BLOCK, seff, x, bx_o, at, final_o)


def out_kernel(
    batches, span, width,
    mixed, conv, spre, marks, bx, cx, state_in, at, skip,
    scanned_o, gated_o,
    seff, x,
):
    blocks = width // BLOCK
    step = softplus(spre[...])
    seff[...] = step + marks[:, 0:1] * STOP
    x[...] = step * conv[...].astype(F32)
    row_ids = lax.broadcasted_iota(jnp.int32, (8, LANES), 0)

    def over_block(i, carry):
        rate = [at[:, tile_at(i, lt)] for lt in range(TILES)]

        def chunk(tc, states):
            states = list(states)
            for b in range(batches):
                rows = pl.ds(pl.multiple_of(b * span + tc * 8, 8), 8)
                for lt in range(TILES):
                    s8 = seff[rows, tile_at(i, lt)]
                    x8 = x[rows, tile_at(i, lt)]
                    h = states[b * TILES + lt]
                    parts = []
                    for j in range(8):
                        t = b * span + tc * 8 + j
                        decay = jnp.exp2(s8[j : j + 1] * rate[lt])
                        h = decay * h + x8[j : j + 1] * bx[t]
                        parts.append(halves(h * cx[t]))
                    states[b * TILES + lt] = h
                    scanned_o[rows, tile_at(i, lt)] = fold_rows(parts, row_ids)
            return tuple(states)

        start = tuple(
            state_in[b, :, tile_at(i, lt)] for b in range(batches) for lt in range(TILES)
        )
        lax.fori_loop(0, span // 8, chunk, start)
        return carry

    lax.fori_loop(0, blocks, over_block, 0)
    scanned = scanned_o[...] + skip[...] * conv[...].astype(F32)
    scanned_o[...] = scanned
    gated_o[...] = (scanned * jax.nn.silu(mixed[:, width:].astype(F32))).astype(BF16)


def back_local_kernel(
    batches, span, width,
    sg, spre, marks, cx, at,
    first_o,
    seff,
):
    blocks = width // BLOCK
    seff[...] = softplus(spre[...]) + marks[:, 0:1] * STOP
    chunks = span // 8

    def over_block(i, carry):
        rate = [at[:, tile_at(i, lt)] for lt in range(TILES)]

        def chunk(k, states):
            states = list(states)
            tc = chunks - 1 - k
            for b in range(batches):
                rows = pl.ds(pl.multiple_of(b * span + tc * 8, 8), 8)
                for lt in range(TILES):
                    s8 = seff[rows, tile_at(i, lt)]
                    g8 = sg[rows, tile_at(i, lt)]
                    q = states[b * TILES + lt]
                    for j in range(7, -1, -1):
                        decay = jnp.exp2(s8[j : j + 1] * rate[lt])
                        q = decay * (q + g8[j : j + 1] * cx[b * span + tc * 8 + j])
                    states[b * TILES + lt] = q
            return tuple(states)

        zero = jnp.zeros((at.shape[0], LANES), F32)
        states = lax.fori_loop(0, chunks, chunk, (zero,) * (batches * TILES))
        for b in range(batches):
            for lt in range(TILES):
                first_o[b, :, tile_at(i, lt)] = states[b * TILES + lt]
        return carry

    lax.fori_loop(0, blocks, over_block, 0)


def back_kernel(
    batches, span, width, rank, states_n,
    sg, spre, pre, conv, mixed, rim, marks, bx, cx, state_in, grad_in, at, skip, cw, xw, dw,
    low_o, pgrad_o, inner_o, spill_o, vec_o,
    seff, x, hist, decays, drive, zsum, acc_b, acc_c, ext,
):
    blocks = width // BLOCK
    rows_n = batches * span
    chunks = span // 8
    m = marks[...]
    step = softplus(spre[...])
    seff[...] = step + m[:, 0:1] * STOP
    x[...] = step * conv[...].astype(F32)
    acc_b[...] = jnp.zeros_like(acc_b)
    acc_c[...] = jnp.zeros_like(acc_c)
    row_ids = lax.broadcasted_iota(jnp.int32, (8, LANES), 0)

    def over_block(i, carry):
        rate = [at[:, tile_at(i, lt)] for lt in range(TILES)]

        def again(tc, states):
            states = list(states)
            for b in range(batches):
                rows = pl.ds(pl.multiple_of(b * span + tc * 8, 8), 8)
                for lt in range(TILES):
                    s8 = seff[rows, tile_at(i, lt)]
                    x8 = x[rows, tile_at(i, lt)]
                    h = states[b * TILES + lt]
                    lanes = pl.ds(lt * LANES, LANES)
                    for j in range(8):
                        t = tc * 8 + j
                        decay = jnp.exp2(s8[j : j + 1] * rate[lt])
                        h = decay * h + x8[j : j + 1] * bx[b * span + t]
                        decays[b, t, :, lanes] = decay
                        hist[b, t + 1, :, lanes] = h
                    states[b * TILES + lt] = h
            return tuple(states)

        for b in range(batches):
            hist[b, 0] = state_in[b, :, block_at(i)]
        start = tuple(
            state_in[b, :, tile_at(i, lt)] for b in range(batches) for lt in range(TILES)
        )
        lax.fori_loop(0, chunks, again, start)

        sums = tuple(jnp.zeros((states_n, LANES), F32) for _ in range(TILES))
        for b in range(batches):

            def chunk(k, held):
                held = list(held)
                tc = chunks - 1 - k
                rows = pl.ds(pl.multiple_of(b * span + tc * 8, 8), 8)
                s8, x8, g8 = [], [], []
                for lt in range(TILES):
                    s8.append(seff[rows, tile_at(i, lt)])
                    x8.append(x[rows, tile_at(i, lt)])
                    g8.append(sg[rows, tile_at(i, lt)])
                drives = [[None] * 8 for _ in range(TILES)]
                zs = [[None] * 8 for _ in range(TILES)]
                for j in range(7, -1, -1):
                    t = tc * 8 + j
                    part_b, part_c = [], []
                    for lt in range(TILES):
                        lanes = pl.ds(lt * LANES, LANES)
                        total = held[lt] + g8[lt][j : j + 1] * cx[b * span + t]
                        q = decays[b, t, :, lanes] * total
                        log_grad = q * hist[b, t, :, lanes]
                        held[TILES + lt] = held[TILES + lt] + log_grad * s8[lt][j : j + 1]
                        zs[lt][j] = halves(log_grad * rate[lt])
                        drives[lt][j] = halves(total * bx[b * span + t])
                        part_b.append(total * x8[lt][j : j + 1])
                        part_c.append(g8[lt][j : j + 1] * hist[b, t + 1, :, lanes])
                        held[lt] = q
                    acc_b[b * span + t] += sum(part_b[1:], part_b[0])
                    acc_c[b * span + t] += sum(part_c[1:], part_c[0])
                for lt in range(TILES):
                    drive[rows, tile_at(i, lt)] = fold_rows(drives[lt], row_ids)
                    zsum[rows, tile_at(i, lt)] = fold_rows(zs[lt], row_ids)
                return tuple(held)

            start = tuple(grad_in[b, :, tile_at(i, lt)] for lt in range(TILES)) + sums
            sums = lax.fori_loop(0, chunks, chunk, start)[TILES:]
        for lt in range(TILES):
            vec_o[0:states_n, tile_at(i, lt)] = -sums[lt]
        return carry

    lax.fori_loop(0, blocks, over_block, 0)

    column_ids = lax.broadcasted_iota(jnp.int32, (states_n, rows_n), 1)

    def gather_column(t, pair):
        now = []
        for held, acc in zip(pair, (acc_b, acc_c)):
            column = jnp.sum(acc[t], axis=1, keepdims=True)
            now.append(jnp.where(column_ids == t, column, held))
        return tuple(now)

    zero = jnp.zeros((states_n, rows_n), F32)
    b_grad, c_grad = lax.fori_loop(0, rows_n, gather_column, (zero, zero), unroll=8)
    placed = jnp.concatenate(
        [
            jnp.zeros((rank, rows_n), F32),
            b_grad,
            c_grad,
            jnp.zeros((LANES - rank - 2 * states_n, rows_n), F32),
        ],
        0,
    ).T
    conv_f = conv[...].astype(F32)
    step = softplus(spre[...])
    step_grad = zsum[...] * (1.0 / LOG2E) + drive[...] * conv_f
    pre_g = step_grad * jax.nn.sigmoid(spre[...])
    low = pre_g.astype(BF16)
    low_o[...] = low
    pgrad = (against(low, dw[...]) + placed).astype(BF16)
    pgrad_o[...] = pgrad
    conv_grad = sg[...] * skip[...] + step * drive[...] + against(pgrad, xw[...])
    pre_grad = conv_grad * silu_slope(pre[...])
    vec_o[states_n + 4 : states_n + 5] = jnp.sum(pre_grad, axis=0, keepdims=True)
    vec_o[states_n + 5 : states_n + 6] = jnp.sum(pre_g, axis=0, keepdims=True)
    vec_o[states_n + 6 : states_n + 7] = jnp.sum(sg[...] * conv_f, axis=0, keepdims=True)
    vec_o[states_n + 7 : states_n + 8] = jnp.zeros((1, width), F32)
    taps = [jnp.zeros((1, width), F32) for _ in range(4)]
    for b in range(batches):
        lo, hi = b * span, (b + 1) * span
        ext[0:8] = rim[b]
        ext[8 : 8 + span] = mixed[lo:hi, :width].astype(F32)
        grad_b = pre_grad[lo:hi]
        taps[3] = taps[3] + jnp.sum(grad_b * ext[8 : 8 + span], axis=0, keepdims=True)
        for k in (1, 2, 3):
            taps[3 - k] = taps[3 - k] + jnp.sum(
                grad_b * (m[lo:hi, k : k + 1] * ext[8 - k : 8 - k + span]),
                axis=0, keepdims=True,
            )
        back = cw[3:4] * grad_b
        spill = jnp.zeros((8, width), F32)
        for k in (1, 2, 3):
            ext[0:8] = jnp.zeros((8, width), F32)
            ext[8 : 8 + span] = cw[3 - k : 4 - k] * (m[lo:hi, k : k + 1] * grad_b)
            ext[8 + span : 16 + span] = jnp.zeros((8, width), F32)
            back = back + ext[8 + k : 8 + k + span]
            spill = spill + ext[k : 8 + k]
        inner_o[lo:hi] = back
        spill_o[b] = spill
    for k in range(4):
        vec_o[states_n + k : states_n + k + 1] = taps[k]


def run(kernel, outs, scratch, *args, flops=0):
    return pl.pallas_call(
        kernel,
        out_shape=[jax.ShapeDtypeStruct(*o) for o in outs],
        in_specs=[pl.BlockSpec(memory_space=pltpu.VMEM)] * len(args),
        out_specs=[pl.BlockSpec(memory_space=pltpu.VMEM)] * len(outs),
        scratch_shapes=[pltpu.VMEM(*s) for s in scratch],
        compiler_params=pltpu.CompilerParams(vmem_limit_bytes=VMEM_LIMIT),
    )(*args)


def flip(array, axis, bit):
    count = lax.axis_size(axis)
    return lax.ppermute(array, axis, [(i, i ^ bit) for i in range(count)])


def shifted(array, by):
    count = lax.axis_size("seq")
    pairs = [(i, i + by) for i in range(count) if 0 <= i + by < count]
    return lax.ppermute(array, "seq", pairs)


def bits_of(count):
    bits = [1 << k for k in range(count.bit_length() - 1)]
    assert 1 << len(bits) == count
    return bits


def pack_total(total):
    one = total.astype(BF16)
    rest = total - one.astype(F32)
    two = rest.astype(BF16)
    three = (rest - two.astype(F32)).astype(BF16)
    return jnp.concatenate([one, two, three], 1)


def carry_forward(final, total, at):
    place = lax.axis_index("seq")
    before = jnp.zeros_like(final)
    span = jnp.zeros_like(total)
    spans = []
    for bit in bits_of(lax.axis_size("seq")):
        upper = (place & bit) != 0
        sent = jnp.concatenate([final.astype(BF16), pack_total(total)], 1)
        got = flip(sent, "seq", bit).astype(F32)
        n = at.shape[0]
        their, their_total = got[:, :n], got[:, n : n + 1] + got[:, n + 1 : n + 2] + got[:, n + 2 :]
        spans.append(their_total)
        before = jnp.where(upper, jnp.exp2(span * at) * their + before, before)
        span = jnp.where(upper, span + their_total, span)
        early, late = jnp.where(upper, their, final), jnp.where(upper, final, their)
        late_total = jnp.where(upper, total, their_total)
        final = jnp.exp2(late_total * at) * early + late
        total = total + their_total
    return before, spans


def carry_backward(first, total, spans, at):
    place = lax.axis_index("seq")
    after = jnp.zeros_like(first)
    span = jnp.zeros_like(total)
    for bit, their_total in zip(bits_of(lax.axis_size("seq")), spans):
        lower = (place & bit) == 0
        their = flip(first.astype(BF16), "seq", bit).astype(F32)
        after = jnp.where(lower, jnp.exp2(span * at) * their + after, after)
        span = jnp.where(lower, span + their_total, span)
        early, late = jnp.where(lower, first, their), jnp.where(lower, their, first)
        early_total = jnp.where(lower, total, their_total)
        first = jnp.exp2(early_total * at) * late + early
        total = total + their_total
    return after


def pick(array, index, axis):
    return lax.dynamic_index_in_dim(array, index, axis, keepdims=False)


def scatter_sum(parts):
    core, place = lax.axis_index("section"), lax.axis_index("seq")
    got = flip(pick(parts, 1 - core, 1), "section", 1)
    total = pick(parts, core, 1).astype(F32) + got.astype(F32)
    bits = bits_of(lax.axis_size("seq"))
    total = total.astype(BF16).reshape((2,) * len(bits) + total.shape[1:])
    left = len(bits)
    for k, bit in enumerate(bits):
        axis = left - 1
        mine = (place // bit) % 2
        got = flip(pick(total, 1 - mine, axis), "seq", bit)
        total = pick(total, mine, axis).astype(F32) + got.astype(F32)
        if k < len(bits) - 1:
            total = total.astype(BF16)
        left -= 1
    return total


def all_sum(parts):
    parts = parts + flip(parts, "section", 1)
    for bit in bits_of(lax.axis_size("seq")):
        parts = parts + flip(parts, "seq", bit)
    return parts


def local(
    tokens, starts, norm_gain, in_weight, conv_weight, conv_bias, xproj_weight,
    dtproj_weight, dt_bias, decay_rate, skip_gain, out_weight, cotangent,
):
    core = lax.axis_index("section")
    place = lax.axis_index("seq")
    cores = lax.axis_size("section")
    count = lax.axis_size("seq")
    batch_count, span, model = tokens.shape
    width = conv_weight.shape[2]
    states_n = decay_rate.shape[2]
    rank = dtproj_weight.shape[1]
    batches = batch_count // cores
    rows_n = batches * span
    low_core = core == 0

    own = (
        norm_gain[0][None], in_weight[0], conv_weight[0], conv_bias[0][None],
        jnp.pad(xproj_weight[0], ((0, 0), (0, LANES - xproj_weight.shape[2]))),
        jnp.pad(dtproj_weight[0], ((0, LANES - rank), (0, 0))),
        dt_bias[0][None], decay_rate[0].T * -LOG2E, skip_gain[0][None], out_weight[0],
    )
    other = tuple(flip(w, "section", 1) for w in own)
    layer_w = (
        tuple(jnp.where(low_core, a, b) for a, b in zip(own, other)),
        tuple(jnp.where(low_core, b, a) for a, b in zip(own, other)),
    )

    def mine(array):
        return lax.dynamic_slice_in_dim(array, core * batches, batches, 0).reshape(
            (rows_n,) + array.shape[2:]
        )

    rows0 = mine(tokens)
    top = mine(cotangent)
    r = lax.dynamic_slice_in_dim(starts, core * batches, batches, 0).astype(F32)
    r_ext = jnp.concatenate([shifted(r[:, -3:].astype(BF16), 1).astype(F32), r], 1)
    free = 1.0 - r_ext
    m1 = free[:, 3:]
    m2 = m1 * free[:, 2:-1]
    m3 = m2 * free[:, 1:-2]
    marks = jnp.stack([r, m1, m2, m3], -1).reshape(rows_n, 4)

    def front(rows, w):
        normed = norm_rows(rows.astype(F32), w[0]).astype(BF16)
        mixed = dot(normed, w[1]).astype(BF16)
        tail = mixed.reshape(batches, span, 2 * width)[:, -3:, :width]
        rim = jnp.pad(shifted(tail, 1).astype(F32), ((0, 0), (5, 0), (0, 0)))
        pre, conv, proj, spre, bx, cx, final, total = run(
            functools.partial(front_kernel, batches, span, width, rank, states_n),
            [
                ((rows_n, width), F32), ((rows_n, width), BF16), ((rows_n, LANES), BF16),
                ((rows_n, width), F32), ((rows_n, states_n, LANES), F32),
                ((rows_n, states_n, LANES), F32), ((batches, states_n, width), F32),
                ((batches, 1, width), F32),
            ],
            [
                ((batches, span + 8, width), F32), ((rows_n, width), F32),
                ((rows_n, width), F32),
            ],
            mixed, rim, marks, w[2], w[3], w[4], w[5], w[6], w[7],
        )
        before, spans = carry_forward(final, total, w[7])
        scanned, gated = run(
            functools.partial(out_kernel, batches, span, width),
            [((rows_n, width), F32), ((rows_n, width), BF16)],
            [((rows_n, width), F32), ((rows_n, width), F32)],
            mixed, conv, spre, marks, bx, cx, before, w[7], w[8],
        )
        result = (rows.astype(F32) + dot(gated, w[9])).astype(BF16)
        kept = (rows, normed, mixed, rim, pre, conv, proj, spre, bx, cx, before, total, spans,
                scanned, gated)
        return result, kept

    def back(g, w, kept):
        (rows, normed, mixed, rim, pre, conv, proj, spre, bx, cx, before, total, spans,
         scanned, gated) = kept
        gated_grad = against(g, w[9])
        gate = mixed[:, width:].astype(F32)
        sg = gated_grad * jax.nn.silu(gate)
        gate_grad = gated_grad * scanned * silu_slope(gate)
        first, = run(
            functools.partial(back_local_kernel, batches, span, width),
            [((batches, states_n, width), F32)],
            [((rows_n, width), F32)],
            sg, spre, marks, cx, w[7],
        )
        after = carry_backward(first, total, spans, w[7])
        low, pgrad, inner, spill, vec = run(
            functools.partial(back_kernel, batches, span, width, rank, states_n),
            [
                ((rows_n, width), BF16), ((rows_n, LANES), BF16), ((rows_n, width), F32),
                ((batches, 8, width), F32), ((states_n + 8, width), F32),
            ],
            [
                ((rows_n, width), F32), ((rows_n, width), F32),
                ((batches, span + 1, states_n, BLOCK), F32),
                ((batches, span, states_n, BLOCK), F32),
                ((rows_n, width), F32), ((rows_n, width), F32),
                ((rows_n, states_n, LANES), F32), ((rows_n, states_n, LANES), F32),
                ((span + 16, width), F32),
            ],
            sg, spre, pre, conv, mixed, rim, marks, bx, cx, before, after, w[7], w[8], w[2],
            w[4], w[5],
        )
        got = shifted(spill[:, 5:], -1)
        inner = inner.reshape(batches, span, width) + jnp.pad(
            got, ((0, 0), (span - 3, 0), (0, 0))
        )
        mixed_grad = jnp.concatenate(
            [inner.reshape(rows_n, width).astype(BF16), gate_grad.astype(BF16)], 1
        )
        normed_grad = against(mixed_grad, w[1])
        source = rows.astype(F32)
        input_grad, grad_gain = jax.vjp(norm_rows, source, w[0])[1](normed_grad)
        low_rows = (g.astype(F32) + input_grad).astype(BF16)
        half = lambda a: a.reshape(count, 2, a.shape[0] // (2 * count), a.shape[1])
        grad_in = half(across(mixed_grad, normed).astype(BF16))
        grad_out = half(across(gated, g).astype(BF16))
        grad_x = across(conv, pgrad)
        grad_dt = across(low, proj)
        columns = lax.broadcasted_iota(jnp.int32, (1, LANES), 1)
        small = jnp.where(
            columns < xproj_weight.shape[2], grad_x, jnp.roll(grad_dt, LANES - rank, 1)
        ).astype(BF16)
        small = small.reshape(count, 2, -1, LANES)
        grad_gain = jnp.pad(grad_gain, ((0, 0), (0, width - model)))
        vec = jnp.concatenate([vec[: states_n + 7], grad_gain], 0)
        return low_rows, (grad_in, grad_out, small, vec)

    def reduce(parts):
        grad_in, grad_out, small, vec = parts
        return scatter_sum(grad_in), scatter_sum(grad_out), scatter_sum(small), all_sum(vec)

    rows1, kept0 = front(rows0, layer_w[0])
    out1, kept1 = front(rows1, layer_w[1])
    g0, parts1 = back(top, layer_w[1], kept1)
    sums1 = reduce(parts1)
    dx, parts0 = back(g0, layer_w[0], kept0)
    sums0 = reduce(parts0)

    def settle(zero, one):
        got = flip(jnp.where(low_core, one, zero), "section", 1)
        own = jnp.where(low_core, zero, one)
        both = jnp.where(low_core, jnp.stack([own, got]), jnp.stack([got, own]))
        return both.reshape((-1,) + own.shape[1:])

    grad_in, grad_out, small = (settle(a, b) for a, b in zip(sums0[:3], sums1[:3]))
    vec = jnp.where(low_core, sums0[3], sums1[3])
    part = width // count
    vec_own = lax.dynamic_slice_in_dim(vec, place * part, part, 1)
    gain_part = model // count
    gain = lax.dynamic_slice_in_dim(vec[states_n + 7], place * gain_part, gain_part, 0)

    got = flip(jnp.where(low_core, out1, dx), "section", 1)
    boundary = jnp.where(
        low_core, jnp.concatenate([dx, got], 0), jnp.concatenate([got, out1], 0)
    ).reshape(1, batch_count, span, model)
    x_width = xproj_weight.shape[2]
    return (
        boundary,
        gain[None],
        grad_in.T[None],
        vec_own[states_n : states_n + 4][None],
        vec_own[states_n + 4][None],
        small[:, :x_width][None],
        small[:, x_width:].T[None],
        vec_own[states_n + 5][None],
        vec_own[:states_n].T[None],
        vec_own[states_n + 6][None],
        grad_out[None],
    )


def solution(mesh):
    in_specs = (
        P(None, "seq", None), P(None, "seq"), P("section", None), P("section", None, None),
        P("section", None, None), P("section", None), P("section", None, None),
        P("section", None, None), P("section", None), P("section", None, None),
        P("section", None), P("section", None, None), P(None, "seq", None),
    )
    out_specs = (
        P("section", None, "seq", None), P("section", "seq"), P("section", None, "seq"),
        P("section", None, "seq"), P("section", "seq"), P("section", "seq", None),
        P("section", None, "seq"), P("section", "seq"), P("section", "seq", None),
        P("section", "seq"), P("section", "seq", None),
    )
    return jax.shard_map(local, mesh=mesh, in_specs=in_specs, out_specs=out_specs, check_vma=False)
```

time: 6050 us -> 446 us (0.07); the launches traced: 5970 us -> 438 us
  local copies, waits for them, and re-layouts: 2440 us -> 20.4 us
  other arithmetic: 1320 us -> 44 us
  blocking collectives: 1140 us -> 0 us
  waiting for transfers between devices: 732 us -> 154 us
  matrix products: 212 us -> 41.1 us
  Pallas kernels: 0 us -> 85.3 us
    pad x300 -> x2, local copies, waits for them, and re-layouts: 2150 us -> 1.02 us  [the longest x1 0.94 us: local(): jnp.pad(dtproj_weight[0], ((0, LANES - rank), (0, 0)))]
    all_gather x25 -> x0, blocking collectives: 1070 us -> none  [the longest x15 631 us: carried_in(): lax.all_gather(part.astype(kind), axis)]
    add x245 -> x9, other arithmetic: 521 us -> 1.98 us  [the longest x6 1.92 us: all_sum(): parts = parts + flip(parts, 'seq', bit)]
    unnamed x10 -> x0, waiting for transfers between devices: 401 us -> none
    reduce_scatter x2 -> x0, waiting for transfers between devices: 317 us -> none  [the longest x1 177 us: spread_end(): lax.psum_scatter(grads[1], 'seq', scatter_dimension=1, tiled=True)]
    mul x130 -> x2, other arithmetic: 263 us -> 0.98 us  [the longest x1 0.91 us: local(): decay_rate[0].T * -LOG2E]
    select_n x240 -> x24, other arithmetic: 210 us -> 12.2 us  [the longest x7 4.55 us: local(): jnp.where(low_core, b, a)]
    concatenate x145 -> x10, other arithmetic: 181 us -> 0.45 us  [the longest x8 0.42 us: carry_forward(): sent = jnp.concatenate([final.astype(BF16), pack_total(total)], 1)]
  transfers between devices with their start and end apart: 41 -> 75, of which waited for: 16 -> 37; matrix products, arithmetic and copies ran while one was open for 1% -> 18% of each run, Pallas kernels for 0% -> 13%
where the time goes in v1:
time: 446 us; the launch traced here: 438 us
  waiting for transfers between devices  154 us (35%)
  starting transfers between devices  90 us (20%)
  Pallas kernels  85.3 us (19%)
  other arithmetic  44 us (10%)
  matrix products  41.1 us (9%)
  local copies, waits for them, and re-layouts  20.4 us (5%)
    ppermute x70, waiting for transfers between devices, flip(): return lax.ppermute(array, axis, [(i, i ^ bit) for i in range(count)])  150 us
    pallas_call x8, Pallas kernels, run(): pl.pallas_call(kernel, out_shape=[jax.ShapeDtypeStruct(*o) for o in outs]...  85.3 us
    ppermute x70, starting transfers between devices, flip(): return lax.ppermute(array, axis, [(i, i ^ bit) for i in range(count)])  76.2 us
    dot_general x4, matrix products, against(): lax.dot_general(left, right, (((1,), (1,)), ((), ())), preferred_element_...  16.1 us
    dot_general x4, matrix products, dot(): return jnp.dot(left, right, preferred_element_type=F32)  14 us
    ppermute x5, starting transfers between devices, shifted(): return lax.ppermute(array, 'seq', pairs)  13.8 us
    dot_general x8, matrix products, across(): lax.dot_general(left, right, (((0,), (0,)), ((), ())), preferred_element_...  11 us
    convert_element_type x6, other arithmetic, scatter_sum(): total = total.astype(BF16).reshape((2,) * len(bits) + total.shape[1:])  9.04 us
  transfers between devices with their start and end apart: 75, of which 37 were waited for; matrix products, arithmetic and copies ran while one was open for 18% of the time, Pallas kernels for 13%

profile of v1, /device:TPU:0, one launch (start us, length us, event | category | flops | bytes accessed | tf_op | source)
XLA Modules:
  0.0 437.8 jit_solution(13590727097264686544)
XLA Ops:
  2.1 4.8 %collective-permute-start.4 = (bf16[2,3]{1,0:T(2,128)(2,1)S(1)}, bf16[2,3]{1,0:T(2,128)(2,1)S(1)}, u32[]{:S(2)}, u32[]{:S(2)}) collective-permute-start(bf16[2,3]{1,0:T(2,128)(2,1)S(1)} %slice.160), channel_id=1, source_target_pairs={{0,1},{1,2},{2,3},{3,4},{4,5},{5,6},{6,7},{7,8},{8,9},{9,10},{10,1... | collective-permute-start | bytes 44 | tf_op jit(solution)/shard_map/ppermute | solution.py:391
  18.3 3.4 convolution_convert_fusion.3.mixed
  21.8 3.5 collective-permute-start.3
  27.5 8.1 %shard_map.212 = (f32[128,1536]{1,0:T(8,128)}, bf16[128,1536]{1,0:T(8,128)(2,1)}, bf16[128,128]{1,0:T(8,128)(2,1)}, f32[128,1536]{1,0:T(8,128)}, f32[128,16,128]...) custom-call(bf16[128,3072]{1,0:T(8,128)(2,1)} %copy-done.10, ...), custom_call_target="tpu_custom_call" | custom-call | tf_op jit(solution)/shard_map/pallas_call | solution.py:373
  37.4 2.4 collective-permute-start.11
  40.3 4.0 collective-permute-done.11
  46.9 2.7 collective-permute-start.12
  49.7 3.7 collective-permute-done.12
  53.7 2.7 collective-permute-start.13
  57.1 2.5 collective-permute-done.13
  59.9 3.1 collective-permute-start.14
  63.0 4.8 %collective-permute-done.14 = bf16[2,19,1536]{2,1,0:T(8,128)(2,1)S(1)} collective-permute-done((bf16[2,19,1536]{2,1,0:T(8,128)(2,1)S(1)}, bf16[2,19,1536]{2,1,0:T(8,128)(2,1)S(1)}, u32[]{:S(2)}, u32[]{:S(2)}) %collective-permute-start.14) | collective-permute-done | bytes 116768 | tf_op jit(solution)/shard_map/ppermute | solution.py:385
  68.6 8.2 %shard_map.213 = (f32[128,1536]{1,0:T(8,128)}, bf16[128,1536]{1,0:T(8,128)(2,1)}) custom-call(bf16[128,3072]{1,0:T(8,128)(2,1)} %copy-done.10, bf16[128,1536]{1,0:T(8,128)(2,1)} %get-tuple-element.41.conv, f32[128,1536]{1,0:T(8,128)} %get-tuple-element.42.spre, f32[128,4]{1,0:T(8,128)} %copy.88.marks, f32[128,16,128]{2,1,0:T(8,128)} %get-tuple-element.43.bx, ...), custom_call_target="tpu_custom_call" | custom-call | tf_op jit(solution)/shard_map/pallas_call | solution.py:373
  76.8 2.5 multiply_reduce_fusion.2
  79.3 5.0 %convolution_convert_fusion.2.mixed = bf16[128,3072]{1,0:T(8,128)(2,1)S(1)} fusion(bf16[768,3072]{1,0:T(8,128)(2,1)} %collective-permute-done.2, pred[]{:T(512)S(6)} %eq.44, bf16[1,768,3072]{2,1,0:T(8,128)(2,1)} %param.16, f32[128,768]{1,0:T(8,128)S(1)} %get-tuple-element.227, f32[768]{0:T(1024)S(1)} %get-tuple-element.108, f32[128]{0:T(128)S(1)} %fusion.96), kind=kOutput, calls=%fused_computation.8 | convolution fusion | flops 607027200 | bytes 10620417 | tf_op jit(solution)/shard_map/dot_general | solution.py:21
  84.4 2.2 collective-permute-start.16
  88.6 8.1 %shard_map.214 = (f32[128,1536]{1,0:T(8,128)}, bf16[128,1536]{1,0:T(8,128)(2,1)}, bf16[128,128]{1,0:T(8,128)(2,1)}, f32[128,1536]{1,0:T(8,128)}, f32[128,16,128]...) custom-call(bf16[128,3072]{1,0:T(8,128)(2,1)} %copy-done.12, ...), custom_call_target="tpu_custom_call" | custom-call | tf_op jit(solution)/shard_map/pallas_call | solution.py:373
  98.5 2.4 collective-permute-start.17
  100.9 3.1 collective-permute-done.17
  106.6 3.8 collective-permute-start.18
  110.4 3.1 collective-permute-done.18
  113.9 3.0 collective-permute-start.19
  116.9 3.4 collective-permute-done.19
  120.6 3.1 collective-permute-start.20
  123.8 4.6 %collective-permute-done.20 = bf16[2,19,1536]{2,1,0:T(8,128)(2,1)S(1)} collective-permute-done((bf16[2,19,1536]{2,1,0:T(8,128)(2,1)S(1)}, bf16[2,19,1536]{2,1,0:T(8,128)(2,1)S(1)}, u32[]{:S(2)}, u32[]{:S(2)}) %collective-permute-start.20) | collective-permute-done | bytes 116768 | tf_op jit(solution)/shard_map/ppermute | solution.py:385
  129.3 8.3 %shard_map.217 = (f32[128,1536]{1,0:T(8,128)}, bf16[128,1536]{1,0:T(8,128)(2,1)}) custom-call(bf16[128,3072]{1,0:T(8,128)(2,1)} %copy-done.12, bf16[128,1536]{1,0:T(8,128)(2,1)} %get-tuple-element.50.conv, f32[128,1536]{1,0:T(8,128)} %get-tuple-element.48.spre, f32[128,4]{1,0:T(8,128)} %copy.88.marks, f32[128,16,128]{2,1,0:T(8,128)} %get-tuple-element.51.bx, ...), custom_call_target="tpu_custom_call" | custom-call | tf_op jit(solution)/shard_map/pallas_call | solution.py:373
  137.6 4.7 %fusion.22 = (f32[128,1536]{1,0:T(8,128)}, bf16[128,1536]{1,0:T(8,128)(2,1)}) fusion(bf16[128,3072]{1,0:T(8,128)(2,1)S(1)} %copy-done.13, f32[128,1536]{1,0:T(8,128)} %get-tuple-element.57, bf16[128,768]{1,0:T(8,128)(2,1)S(1)} %bitcast.420, bf16[1536,768]{1,0:T(8,128)(2,1)} %collective-permute-done, pred[]{:T(512)S(6)} %eq.44, bf16[1,1536,768]{2,1,0:T(8,128)(2,1)} %param.24), kind=kOutput, calls=%fused_computation.60 | convolution fusion | flops 305725440 | bytes 7274497 | tf_op jit(solution)/shard_map/dot_general | solution.py:29
  142.2 5.7 %shard_map.215 = f32[2,16,1536]{2,1,0:T(8,128)} custom-call(f32[128,1536]{1,0:T(8,128)} %get-tuple-element.160.sg, f32[128,1536]{1,0:T(8,128)} %get-tuple-element.48.spre, f32[128,4]{1,0:T(8,128)} %copy.88.marks, f32[128,16,128]{2,1,0:T(8,128)} %get-tuple-element.52.cx, f32[16,1536]{1,0:T(8,128)} %get-tuple-element.132.at), custom_call_target="tpu_custom_call" | custom-call | tf_op jit(solution)/shard_map/pallas_call | solution.py:373
  149.1 4.5 %collective-permute-done.21 = bf16[2,16,1536]{2,1,0:T(8,128)(2,1)S(1)} collective-permute-done((bf16[2,16,1536]{2,1,0:T(8,128)(2,1)S(1)}, bf16[2,16,1536]{2,1,0:T(8,128)(2,1)S(1)}, u32[]{:S(2)}, u32[]{:S(2)}) %collective-permute-start.21) | collective-permute-done | bytes 98336 | tf_op jit(solution)/shard_map/ppermute | solution.py:385
  155.5 3.9 collective-permute-done.22
  162.3 2.8 collective-permute-done.23
  165.3 2.4 collective-permute-start.24
  168.8 3.1 collective-permute-done.24
  172.8 20.6 %shard_map.216 = (bf16[128,1536]{1,0:T(8,128)(2,1)}, bf16[128,128]{1,0:T(8,128)(2,1)}, f32[128,1536]{1,0:T(8,128)}, f32[2,8,1536]{2,1,0:T(8,128)}, f32[24,1536]{1,0:T(8,128)}) custom-call(f32[128,1536]{1,0:T(8,128)} %get-tuple-element.160.sg, f32[128,1536]{1,0:T(8,128)} %get-tuple-element.48.spre, f32[128,1536]{1,0:T(8,128)} %get-tuple-element.49.pre, ...), custom_call_target="tpu_custom_call" | custom-call | tf_op jit(solution)/shard_map/pallas_call | solution.py:373
  202.7 5.9 %multiply_reduce_fusion = (f32[768]{0:T(1024)S(1)}, f32[128]{0:T(128)S(1)}, f32[128,768]{1,0:T(8,128)S(1)}) fusion(f32[128,768]{1,0:T(8,128)S(1)} %get-tuple-element.227, f32[128]{0:T(128)S(1)} %fusion.96, f32[768]{0:T(1024)S(1)} %get-tuple-element.108, bf16[768,3072]{1,0:T(8,128)(2,1)} %collective-permute-done.2, pred[]{:T(512)S(6)} %eq.44, ...), kind=kOutput, calls=%fused_computation.113 | convolution fusion | flops 608500864 | bytes 11017217 | tf_op jit(solution)/shard_map/dot_general | solution.py:29
  208.8 2.3 convolution_convert_fusion.5
  211.1 3.8 fusion.30
  214.8 5.7 %shard_map.218 = f32[2,16,1536]{2,1,0:T(8,128)} custom-call(f32[128,1536]{1,0:T(8,128)} %get-tuple-element.158.sg, f32[128,1536]{1,0:T(8,128)} %get-tuple-element.42.spre, f32[128,4]{1,0:T(8,128)} %copy.88.marks, f32[128,16,128]{2,1,0:T(8,128)} %get-tuple-element.44.cx, f32[16,1536]{1,0:T(8,128)} %get-tuple-element.177.at), custom_call_target="tpu_custom_call" | custom-call | tf_op jit(solution)/shard_map/pallas_call | solution.py:373
  230.2 4.1 collective-permute-done.59
  236.3 3.1 collective-permute-done.38
  241.1 3.1 collective-permute-done.28
  244.7 3.4 collective-permute-done.61
  248.0 2.2 collective-permute-start.29
  250.2 4.2 collective-permute-done.29
  255.3 20.6 %shard_map.219 = (bf16[128,1536]{1,0:T(8,128)(2,1)}, bf16[128,128]{1,0:T(8,128)(2,1)}, f32[128,1536]{1,0:T(8,128)}, f32[2,8,1536]{2,1,0:T(8,128)}, f32[24,1536]{1,0:T(8,128)}) custom-call(f32[128,1536]{1,0:T(8,128)} %get-tuple-element.158.sg, f32[128,1536]{1,0:T(8,128)} %get-tuple-element.42.spre, f32[128,1536]{1,0:T(8,128)} %get-tuple-element.58.pre, ...), custom_call_target="tpu_custom_call" | custom-call | tf_op jit(solution)/shard_map/pallas_call | solution.py:373
  286.3 3.1 broadcast_select_fusion.16
  293.2 3.6 collective-permute-start.32
  298.2 2.2 collective-permute-start.55
  300.4 2.9 collective-permute-done.40
  307.0 2.7 collective-permute-done.33
  314.4 2.3 collective-permute-start.34
  323.2 4.4 %collective-permute-done.35 = f32[24,1536]{1,0:T(8,128)} collective-permute-done((f32[24,1536]{1,0:T(8,128)S(1)}, f32[24,1536]{1,0:T(8,128)}, u32[]{:S(2)}, u32[]{:S(2)}) %collective-permute-start.35) | collective-permute-done | bytes 147488 | tf_op jit(solution)/shard_map/ppermute | solution.py:385
  329.2 2.3 collective-permute-start.36
  336.1 3.7 collective-permute-done.41
  343.4 4.2 collective-permute-done.71
  349.7 2.5 fusion
  352.9 2.4 fusion.1
  358.3 2.1 collective-permute-start.73
  360.5 4.1 collective-permute-done.66
  365.7 15.7 %collective-permute-done.48 = bf16[2,2,2,96,768]{4,3,0,1,2:T(8,128)(2,1)S(1)} collective-permute-done((bf16[2,2,2,96,768]{4,3,0,1,2:T(8,128)(2,1)S(1)}, bf16[2,2,2,96,768]{4,3,0,1,2:T(8,128)(2,1)S(1)}, u32[]{:S(2)}, u32[]{:S(2)}) %collective-permute-start.48) | collective-permute-done | bytes 1179680 | tf_op jit(solution)/shard_map/ppermute | solution.py:385
  382.7 21.7 %collective-permute-done.43 = bf16[2,2,2,96,768]{4,3,0,1,2:T(8,128)(2,1)S(1)} collective-permute-done((bf16[2,2,2,96,768]{4,3,0,1,2:T(8,128)(2,1)S(1)}, bf16[2,2,2,96,768]{4,3,0,1,2:T(8,128)(2,1)S(1)}, u32[]{:S(2)}, u32[]{:S(2)}) %collective-permute-start.43) | collective-permute-done | bytes 1179680 | tf_op jit(solution)/shard_map/ppermute | solution.py:385
  408.6 9.5 %collective-permute-done.44 = bf16[2,2,96,768]{3,2,0,1:T(8,128)(2,1)S(1)} collective-permute-done((bf16[2,2,96,768]{3,2,0,1:T(8,128)(2,1)S(1)}, bf16[2,2,96,768]{3,2,0,1:T(8,128)(2,1)S(1)}, u32[]{:S(2)}, u32[]{:S(2)}) %collective-permute-start.44) | collective-permute-done | bytes 589856 | tf_op jit(solution)/shard_map/ppermute | solution.py:385
  420.7 6.7 %collective-permute-done.45 = bf16[2,96,768]{2,1,0:T(8,128)(2,1)S(1)} collective-permute-done((bf16[2,96,768]{2,1,0:T(8,128)(2,1)S(1)}, bf16[2,96,768]{2,1,0:T(8,128)(2,1)S(1)}, u32[]{:S(2)}, u32[]{:S(2)}) %collective-permute-start.45) | collective-permute-done | bytes 294944 | tf_op jit(solution)/shard_map/ppermute | solution.py:385
  427.9 6.7 %collective-permute-done.46 = bf16[96,768]{1,0:T(8,128)(2,1)S(1)} collective-permute-done((bf16[96,768]{1,0:T(8,128)(2,1)S(1)}, bf16[96,768]{1,0:T(8,128)(2,1)S(1)}, u32[]{:S(2)}, u32[]{:S(2)}) %collective-permute-start.46) | collective-permute-done | bytes 147488 | tf_op jit(solution)/shard_map/ppermute | solution.py:385
  (433 shorter events, 119.8 us)
Async XLA Ops:
  0.7 17.6 %collective-permute-start.2 = (bf16[768,3072]{1,0:T(8,128)(2,1)}, bf16[768,3072]{1,0:T(8,128)(2,1)}, u32[]{:S(2)}, u32[]{:S(2)}) collective-permute-start(bf16[768,3072]{1,0:T(8,128)(2,1)} %bitcast.483), channel_id=1, source_target_pairs={{0,16},{16,0},{1,17},{17,1},{2,18},{18,2},{3,19},{19,3},{4,20},{20... | collective-permute-start | bytes 14155784 | tf_op jit(solution)/shard_map/ppermute | solution.py:385
  1.2 11.9 %collective-permute-start.1 = (f32[1,768]{1,0:T(1,128)}, f32[1,768]{1,0:T(1,128)S(1)}, u32[]{:S(2)}, u32[]{:S(2)}) collective-permute-start(f32[1,768]{1,0:T(1,128)} %param.15), channel_id=1, source_target_pairs={{0,16},{16,0},{1,17},{17,1},{2,18},{18,2},{3,19},{19,3},{4,20},{20... | collective-permute-start | bytes 9224 | tf_op jit(solution)/shard_map/ppermute | solution.py:385
  2.1 9.7 %collective-permute-start.4 = (bf16[2,3]{1,0:T(2,128)(2,1)S(1)}, bf16[2,3]{1,0:T(2,128)(2,1)S(1)}, u32[]{:S(2)}, u32[]{:S(2)}) collective-permute-start(bf16[2,3]{1,0:T(2,128)(2,1)S(1)} %slice.160), channel_id=1, source_target_pairs={{0,1},{1,2},{2,3},{3,4},{4,5},{5,6},{6,7},{7,8},{8,9},{9,10},{10,1... | collective-permute-start | bytes 44 | tf_op jit(solution)/shard_map/ppermute | solution.py:391
  6.9 9.0 %collective-permute-start.5 = (f32[4,1536]{1,0:T(4,128)}, f32[4,1536]{1,0:T(4,128)S(1)}, u32[]{:S(2)}, u32[]{:S(2)}) collective-permute-start(f32[4,1536]{1,0:T(4,128)} %bitcast.481), channel_id=1, source_target_pairs={{0,16},{16,0},{1,17},{17,1},{2,18},{18,2},{3,19},{19,3},{4,20},{20... | collective-permute-start | bytes 73736 | tf_op jit(solution)/shard_map/ppermute | solution.py:385
  7.0 6.8 %collective-permute-start.6 = (f32[1,1536]{1,0:T(1,128)}, f32[1,1536]{1,0:T(1,128)S(1)}, u32[]{:S(2)}, u32[]{:S(2)}) collective-permute-start(f32[1,1536]{1,0:T(1,128)} %param.18), channel_id=1, source_target_pairs={{0,16},{16,0},{1,17},{17,1},{2,18},{18,2},{3,19},{19,3},{4,20},{20... | collective-permute-start | bytes 18440 | tf_op jit(solution)/shard_map/ppermute | solution.py:385
  11.8 5.4 %collective-permute-start.7 = (bf16[1536,128]{1,0:T(8,128)(2,1)S(1)}, bf16[1536,128]{1,0:T(8,128)(2,1)S(1)}, u32[]{:S(2)}, u32[]{:S(2)}) collective-permute-start(bf16[1536,128]{1,0:T(8,128)(2,1)S(1)} %pad.35), channel_id=1, source_target_pairs={{0,16},{16,0},{1,17},{17,1},{2,18},{18,2},{3,19},{19,3},{4,20},{20... | collective-permute-start | bytes 1179656 | tf_op jit(solution)/shard_map/ppermute | solution.py:385
  13.1 12.2 %collective-permute-start.8 = (bf16[128,1536]{1,0:T(8,128)(2,1)S(1)}, bf16[128,1536]{1,0:T(8,128)(2,1)S(1)}, u32[]{:S(2)}, u32[]{:S(2)}) collective-permute-start(bf16[128,1536]{1,0:T(8,128)(2,1)S(1)} %pad.36), channel_id=1, source_target_pairs={{0,16},{16,0},{1,17},{17,1},{2,18},{18,2},{3,19},{19,3},{4,20},{20... | collective-permute-start | bytes 1179656 | tf_op jit(solution)/shard_map/ppermute | solution.py:385
  21.8 5.0 %collective-permute-start.3 = (bf16[2,3,1536]{2,1,0:T(4,128)(2,1)S(1)}, bf16[2,3,1536]{2,1,0:T(4,128)(2,1)S(1)}, u32[]{:S(2)}, u32[]{:S(2)}) collective-permute-start(bf16[2,3,1536]{2,1,0:T(4,128)(2,1)S(1)} %slice.211), channel_id=1, source_target_pairs={{0,1},{1,2},{2,3},{3,4},{4,5},{5,6},{6,7},{7,8},{8,9},{9,10},{10,1... | collective-permute-start | bytes 55304 | tf_op jit(solution)/shard_map/ppermute | solution.py:391
  37.4 6.9 %collective-permute-start.11 = (bf16[2,19,1536]{2,1,0:T(8,128)(2,1)S(1)}, bf16[2,19,1536]{2,1,0:T(8,128)(2,1)S(1)}, u32[]{:S(2)}, u32[]{:S(2)}) collective-permute-start(bf16[2,19,1536]{2,1,0:T(8,128)(2,1)S(1)} %pad_maximum_fusion.6), channel_id=1, source_target_pairs={{0,1},{1,0},{2,3},{3,2},{4,5},{5,4},{6,7},{7,6},{8,9},{9,8},{10,11... | collective-permute-start | bytes 350216 | tf_op jit(solution)/shard_map/ppermute | solution.py:385
  39.8 16.7 %collective-permute-start.15 = (f32[1,1536]{1,0:T(1,128)S(1)}, f32[1,1536]{1,0:T(1,128)S(1)}, u32[]{:S(2)}, u32[]{:S(2)}) collective-permute-start(f32[1,1536]{1,0:T(1,128)S(1)} %copy-done.45), channel_id=1, source_target_pairs={{0,16},{16,0},{1,17},{17,1},{2,18},{18,2},{3,19},{19,3},{4,20},{20... | collective-permute-start | bytes 18440 | tf_op jit(solution)/shard_map/ppermute | solution.py:385
  40.0 36.8 %collective-permute-start = (bf16[1536,768]{1,0:T(8,128)(2,1)}, bf16[1536,768]{1,0:T(8,128)(2,1)}, u32[]{:S(2)}, u32[]{:S(2)}) collective-permute-start(bf16[1536,768]{1,0:T(8,128)(2,1)} %bitcast.1), channel_id=1, source_target_pairs={{0,16},{16,0},{1,17},{17,1},{2,18},{18,2},{3,19},{19,3},{4,20},{20... | collective-permute-start | bytes 7077896 | tf_op jit(solution)/shard_map/ppermute | solution.py:385
  46.9 6.5 %collective-permute-start.12 = (bf16[2,19,1536]{2,1,0:T(8,128)(2,1)S(1)}, bf16[2,19,1536]{2,1,0:T(8,128)(2,1)S(1)}, u32[]{:S(2)}, u32[]{:S(2)}) collective-permute-start(bf16[2,19,1536]{2,1,0:T(8,128)(2,1)S(1)} %pad_maximum_fusion.7), channel_id=1, source_target_pairs={{0,2},{1,3},{2,0},{3,1},{4,6},{5,7},{6,4},{7,5},{8,10},{9,11},{10,... | collective-permute-start | bytes 350216 | tf_op jit(solution)/shard_map/ppermute | solution.py:385
  53.7 5.9 %collective-permute-start.13 = (bf16[2,19,1536]{2,1,0:T(8,128)(2,1)S(1)}, bf16[2,19,1536]{2,1,0:T(8,128)(2,1)S(1)}, u32[]{:S(2)}, u32[]{:S(2)}) collective-permute-start(bf16[2,19,1536]{2,1,0:T(8,128)(2,1)S(1)} %pad_maximum_fusion.8), channel_id=1, source_target_pairs={{0,4},{1,5},{2,6},{3,7},{4,0},{5,1},{6,2},{7,3},{8,12},{9,13},{10,... | collective-permute-start | bytes 350216 | tf_op jit(solution)/shard_map/ppermute | solution.py:385
  59.9 7.9 %collective-permute-start.14 = (bf16[2,19,1536]{2,1,0:T(8,128)(2,1)S(1)}, bf16[2,19,1536]{2,1,0:T(8,128)(2,1)S(1)}, u32[]{:S(2)}, u32[]{:S(2)}) collective-permute-start(bf16[2,19,1536]{2,1,0:T(8,128)(2,1)S(1)} %pad_maximum_fusion.9), channel_id=1, source_target_pairs={{0,8},{1,9},{2,10},{3,11},{4,12},{5,13},{6,14},{7,15},{8,0},{9,1},... | collective-permute-start | bytes 350216 | tf_op jit(solution)/shard_map/ppermute | solution.py:385
  98.5 5.5 %collective-permute-start.17 = (bf16[2,19,1536]{2,1,0:T(8,128)(2,1)S(1)}, bf16[2,19,1536]{2,1,0:T(8,128)(2,1)S(1)}, u32[]{:S(2)}, u32[]{:S(2)}) collective-permute-start(bf16[2,19,1536]{2,1,0:T(8,128)(2,1)S(1)} %pad_maximum_fusion.10), channel_id=1, source_target_pairs={{0,1},{1,0},{2,3},{3,2},{4,5},{5,4},{6,7},{7,6},{8,9},{9,8},{10,11... | collective-permute-start | bytes 350216 | tf_op jit(solution)/shard_map/ppermute | solution.py:385
  106.6 6.9 %collective-permute-start.18 = (bf16[2,19,1536]{2,1,0:T(8,128)(2,1)S(1)}, bf16[2,19,1536]{2,1,0:T(8,128)(2,1)S(1)}, u32[]{:S(2)}, u32[]{:S(2)}) collective-permute-start(bf16[2,19,1536]{2,1,0:T(8,128)(2,1)S(1)} %pad_maximum_fusion.11), channel_id=1, source_target_pairs={{0,2},{1,3},{2,0},{3,1},{4,6},{5,7},{6,4},{7,5},{8,10},{9,11},{10,... | collective-permute-start | bytes 350216 | tf_op jit(solution)/shard_map/ppermute | solution.py:385
  113.9 6.5 %collective-permute-start.19 = (bf16[2,19,1536]{2,1,0:T(8,128)(2,1)S(1)}, bf16[2,19,1536]{2,1,0:T(8,128)(2,1)S(1)}, u32[]{:S(2)}, u32[]{:S(2)}) collective-permute-start(bf16[2,19,1536]{2,1,0:T(8,128)(2,1)S(1)} %pad_maximum_fusion.12), channel_id=1, source_target_pairs={{0,4},{1,5},{2,6},{3,7},{4,0},{5,1},{6,2},{7,3},{8,12},{9,13},{10,... | collective-permute-start | bytes 350216 | tf_op jit(solution)/shard_map/ppermute | solution.py:385
  120.6 7.8 %collective-permute-start.20 = (bf16[2,19,1536]{2,1,0:T(8,128)(2,1)S(1)}, bf16[2,19,1536]{2,1,0:T(8,128)(2,1)S(1)}, u32[]{:S(2)}, u32[]{:S(2)}) collective-permute-start(bf16[2,19,1536]{2,1,0:T(8,128)(2,1)S(1)} %pad_maximum_fusion.13), channel_id=1, source_target_pairs={{0,8},{1,9},{2,10},{3,11},{4,12},{5,13},{6,14},{7,15},{8,0},{9,1},... | collective-permute-start | bytes 350216 | tf_op jit(solution)/shard_map/ppermute | solution.py:385
  160.4 4.7 %collective-permute-start.23 = (bf16[2,16,1536]{2,1,0:T(8,128)(2,1)S(1)}, bf16[2,16,1536]{2,1,0:T(8,128)(2,1)S(1)}, u32[]{:S(2)}, u32[]{:S(2)}) collective-permute-start(bf16[2,16,1536]{2,1,0:T(8,128)(2,1)S(1)} %fusion.76), channel_id=1, source_target_pairs={{0,4},{1,5},{2,6},{3,7},{4,0},{5,1},{6,2},{7,3},{8,12},{9,13},{10,... | collective-permute-start | bytes 294920 | tf_op jit(solution)/shard_map/ppermute | solution.py:385
  165.3 6.6 %collective-permute-start.24 = (bf16[2,16,1536]{2,1,0:T(8,128)(2,1)S(1)}, bf16[2,16,1536]{2,1,0:T(8,128)(2,1)S(1)}, u32[]{:S(2)}, u32[]{:S(2)}) collective-permute-start(bf16[2,16,1536]{2,1,0:T(8,128)(2,1)S(1)} %fusion.61), channel_id=1, source_target_pairs={{0,8},{1,9},{2,10},{3,11},{4,12},{5,13},{6,14},{7,15},{8,0},{9,1},... | collective-permute-start | bytes 294920 | tf_op jit(solution)/shard_map/ppermute | solution.py:385
  168.8 142.5 %collective-permute-start.69 = (bf16[16,48,768]{2,1,0:T(8,128)(2,1)}, bf16[16,48,768]{2,1,0:T(8,128)(2,1)}, u32[]{:S(2)}, u32[]{:S(2)}) collective-permute-start(bf16[16,48,768]{2,1,0:T(8,128)(2,1)} %dynamic-slice_bitcast_fusion.2), channel_id=1, source_target_pairs={{0,16},{16,0},{1,17},{17,1},{2,18},{18,2},{3,19},{19,3},{4,20},{20... | collective-permute-start | bytes 3538952 | tf_op jit(solution)/shard_map/ppermute | solution.py:385
  194.4 6.0 %collective-permute-start.25 = (f32[2,3,1536]{2,1,0:T(4,128)S(1)}, f32[2,3,1536]{2,1,0:T(4,128)S(1)}, u32[]{:S(2)}, u32[]{:S(2)}) collective-permute-start(f32[2,3,1536]{2,1,0:T(4,128)S(1)} %slice.194), channel_id=1, source_target_pairs={{1,0},{2,1},{3,2},{4,3},{5,4},{6,5},{7,6},{8,7},{9,8},{10,9},{11,1... | collective-permute-start | bytes 110600 | tf_op jit(solution)/shard_map/ppermute | solution.py:391
  199.3 28.2 %collective-permute-start.58 = (bf16[16,48,128]{2,1,0:T(8,128)(2,1)}, bf16[16,48,128]{2,1,0:T(8,128)(2,1)}, u32[]{:S(2)}, u32[]{:S(2)}) collective-permute-start(bf16[16,48,128]{2,1,0:T(8,128)(2,1)} %dynamic-slice_bitcast_fusion.10), channel_id=1, source_target_pairs={{0,16},{16,0},{1,17},{17,1},{2,18},{18,2},{3,19},{19,3},{4,20},{20... | collective-permute-start | bytes 589832 | tf_op jit(solution)/shard_map/ppermute | solution.py:385
  221.5 5.4 %collective-permute-start.26 = (bf16[2,16,1536]{2,1,0:T(8,128)(2,1)S(1)}, bf16[2,16,1536]{2,1,0:T(8,128)(2,1)S(1)}, u32[]{:S(2)}, u32[]{:S(2)}) collective-permute-start(bf16[2,16,1536]{2,1,0:T(8,128)(2,1)S(1)} %convert_element_type.745), channel_id=1, source_target_pairs={{0,1},{1,0},{2,3},{3,2},{4,5},{5,4},{6,7},{7,6},{8,9},{9,8},{10,11... | collective-permute-start | bytes 294920 | tf_op jit(solution)/shard_map/ppermute | solution.py:385
  223.2 6.3 %collective-permute-start.37 = (f32[24,1536]{1,0:T(8,128)S(1)}, f32[24,1536]{1,0:T(8,128)S(1)}, u32[]{:S(2)}, u32[]{:S(2)}) collective-permute-start(f32[24,1536]{1,0:T(8,128)S(1)} %select_maximum_fusion), channel_id=1, source_target_pairs={{0,16},{16,0},{1,17},{17,1},{2,18},{18,2},{3,19},{19,3},{4,20},{20... | collective-permute-start | bytes 442376 | tf_op jit(solution)/shard_map/ppermute | solution.py:385
  225.0 124.6 %collective-permute-start.47 = (bf16[16,96,768]{2,1,0:T(8,128)(2,1)}, bf16[16,96,768]{2,1,0:T(8,128)(2,1)}, u32[]{:S(2)}, u32[]{:S(2)}) collective-permute-start(bf16[16,96,768]{2,1,0:T(8,128)(2,1)} %dynamic-slice_bitcast_fusion), channel_id=1, source_target_pairs={{0,16},{16,0},{1,17},{17,1},{2,18},{18,2},{3,19},{19,3},{4,20},{20... | collective-permute-start | bytes 7077896 | tf_op jit(solution)/shard_map/ppermute | solution.py:385
  226.9 102.3 %collective-permute-start.64 = (bf16[16,48,768]{2,1,0:T(8,128)(2,1)}, bf16[16,48,768]{2,1,0:T(8,128)(2,1)}, u32[]{:S(2)}, u32[]{:S(2)}) collective-permute-start(bf16[16,48,768]{2,1,0:T(8,128)(2,1)} %dynamic-slice_bitcast_fusion.3), channel_id=1, source_target_pairs={{0,16},{16,0},{1,17},{17,1},{2,18},{18,2},{3,19},{19,3},{4,20},{20... | collective-permute-start | bytes 3538952 | tf_op jit(solution)/shard_map/ppermute | solution.py:385
  227.5 7.5 %collective-permute-start.27 = (bf16[2,16,1536]{2,1,0:T(8,128)(2,1)S(1)}, bf16[2,16,1536]{2,1,0:T(8,128)(2,1)S(1)}, u32[]{:S(2)}, u32[]{:S(2)}) collective-permute-start(bf16[2,16,1536]{2,1,0:T(8,128)(2,1)S(1)} %fusion.111), channel_id=1, source_target_pairs={{0,2},{1,3},{2,0},{3,1},{4,6},{5,7},{6,4},{7,5},{8,10},{9,11},{10,... | collective-permute-start | bytes 294920 | tf_op jit(solution)/shard_map/ppermute | solution.py:385
  234.2 5.1 %collective-permute-start.38 = (f32[24,1536]{1,0:T(8,128)S(1)}, f32[24,1536]{1,0:T(8,128)S(1)}, u32[]{:S(2)}, u32[]{:S(2)}) collective-permute-start(f32[24,1536]{1,0:T(8,128)S(1)} %fusion.146), channel_id=1, source_target_pairs={{0,1},{1,0},{2,3},{3,2},{4,5},{5,4},{6,7},{7,6},{8,9},{9,8},{10,11... | collective-permute-start | bytes 442376 | tf_op jit(solution)/shard_map/ppermute | solution.py:385
  239.4 4.8 %collective-permute-start.28 = (bf16[2,16,1536]{2,1,0:T(8,128)(2,1)S(1)}, bf16[2,16,1536]{2,1,0:T(8,128)(2,1)S(1)}, u32[]{:S(2)}, u32[]{:S(2)}) collective-permute-start(bf16[2,16,1536]{2,1,0:T(8,128)(2,1)S(1)} %fusion.75), channel_id=1, source_target_pairs={{0,4},{1,5},{2,6},{3,7},{4,0},{5,1},{6,2},{7,3},{8,12},{9,13},{10,... | collective-permute-start | bytes 294920 | tf_op jit(solution)/shard_map/ppermute | solution.py:385
  239.7 53.5 %collective-permute-start.39 = (f32[24,1536]{1,0:T(8,128)S(1)}, f32[24,1536]{1,0:T(8,128)S(1)}, u32[]{:S(2)}, u32[]{:S(2)}) collective-permute-start(f32[24,1536]{1,0:T(8,128)S(1)} %add.566), channel_id=1, source_target_pairs={{0,2},{1,3},{2,0},{3,1},{4,6},{5,7},{6,4},{7,5},{8,10},{9,11},{10,... | collective-permute-start | bytes 442376 | tf_op jit(solution)/shard_map/ppermute | solution.py:385
  248.0 6.4 %collective-permute-start.29 = (bf16[2,16,1536]{2,1,0:T(8,128)(2,1)S(1)}, bf16[2,16,1536]{2,1,0:T(8,128)(2,1)S(1)}, u32[]{:S(2)}, u32[]{:S(2)}) collective-permute-start(bf16[2,16,1536]{2,1,0:T(8,128)(2,1)S(1)} %fusion.69), channel_id=1, source_target_pairs={{0,8},{1,9},{2,10},{3,11},{4,12},{5,13},{6,14},{7,15},{8,0},{9,1},... | collective-permute-start | bytes 294920 | tf_op jit(solution)/shard_map/ppermute | solution.py:385
  276.9 6.0 %collective-permute-start.30 = (f32[2,3,1536]{2,1,0:T(4,128)S(1)}, f32[2,3,1536]{2,1,0:T(4,128)S(1)}, u32[]{:S(2)}, u32[]{:S(2)}) collective-permute-start(f32[2,3,1536]{2,1,0:T(4,128)S(1)} %slice.196), channel_id=1, source_target_pairs={{1,0},{2,1},{3,2},{4,3},{5,4},{6,5},{7,6},{8,7},{9,8},{10,9},{11,1... | collective-permute-start | bytes 110600 | tf_op jit(solution)/shard_map/ppermute | solution.py:391
  282.8 6.6 %collective-permute-start.53 = (bf16[16,48,128]{2,1,0:T(8,128)(2,1)S(1)}, bf16[16,48,128]{2,1,0:T(8,128)(2,1)S(1)}, u32[]{:S(2)}, u32[]{:S(2)}) collective-permute-start(bf16[16,48,128]{2,1,0:T(8,128)(2,1)S(1)} %dynamic-slice_bitcast_fusion.11), channel_id=1, source_target_pairs={{0,16},{16,0},{1,17},{17,1},{2,18},{18,2},{3,19},{19,3},{4,20},{20... | collective-permute-start | bytes 589832 | tf_op jit(solution)/shard_map/ppermute | solution.py:385
  289.6 7.2 %collective-permute-start.54 = (bf16[2,2,2,48,128]{4,3,2,1,0:T(8,128)(2,1)S(1)}, bf16[2,2,2,48,128]{4,3,2,1,0:T(8,128)(2,1)S(1)}, u32[]{:S(2)}, u32[]{:S(2)}) collective-permute-start(bf16[2,2,2,48,128]{4,3,2,1,0:T(8,128)(2,1)S(1)} %dynamic-slice_bitcast_fusion.16), channel_id=1, source_target_pairs={{0,1},{1,0},{2,3},{3,2},{4,5},{5,4},{6,7},{7,6},{8,9},{9,8},{10,11... | collective-permute-start | bytes 294920 | tf_op jit(solution)/shard_map/ppermute | solution.py:385
  293.2 5.0 %collective-permute-start.32 = (f32[24,1536]{1,0:T(8,128)S(1)}, f32[24,1536]{1,0:T(8,128)S(1)}, u32[]{:S(2)}, u32[]{:S(2)}) collective-permute-start(f32[24,1536]{1,0:T(8,128)S(1)} %select_maximum_fusion.1), channel_id=1, source_target_pairs={{0,16},{16,0},{1,17},{17,1},{2,18},{18,2},{3,19},{19,3},{4,20},{20... | collective-permute-start | bytes 442376 | tf_op jit(solution)/shard_map/ppermute | solution.py:385
  296.8 6.5 %collective-permute-start.40 = (f32[24,1536]{1,0:T(8,128)S(1)}, f32[24,1536]{1,0:T(8,128)S(1)}, u32[]{:S(2)}, u32[]{:S(2)}) collective-permute-start(f32[24,1536]{1,0:T(8,128)S(1)} %add.567), channel_id=1, source_target_pairs={{0,4},{1,5},{2,6},{3,7},{4,0},{5,1},{6,2},{7,3},{8,12},{9,13},{10,... | collective-permute-start | bytes 442376 | tf_op jit(solution)/shard_map/ppermute | solution.py:385
  298.2 5.2 %collective-permute-start.55 = (bf16[2,2,48,128]{3,2,1,0:T(8,128)(2,1)S(1)}, bf16[2,2,48,128]{3,2,1,0:T(8,128)(2,1)S(1)}, u32[]{:S(2)}, u32[]{:S(2)}) collective-permute-start(bf16[2,2,48,128]{3,2,1,0:T(8,128)(2,1)S(1)} %dynamic-slice_bitcast_fusion.20), channel_id=1, source_target_pairs={{0,2},{1,3},{2,0},{3,1},{4,6},{5,7},{6,4},{7,5},{8,10},{9,11},{10,... | collective-permute-start | bytes 147464 | tf_op jit(solution)/shard_map/ppermute | solution.py:385
  303.4 6.2 %collective-permute-start.33 = (f32[24,1536]{1,0:T(8,128)S(1)}, f32[24,1536]{1,0:T(8,128)S(1)}, u32[]{:S(2)}, u32[]{:S(2)}) collective-permute-start(f32[24,1536]{1,0:T(8,128)S(1)} %fusion.145), channel_id=1, source_target_pairs={{0,1},{1,0},{2,3},{3,2},{4,5},{5,4},{6,7},{7,6},{8,9},{9,8},{10,11... | collective-permute-start | bytes 442376 | tf_op jit(solution)/shard_map/ppermute | solution.py:385
  304.8 6.4 %collective-permute-start.56 = (bf16[2,48,128]{2,1,0:T(8,128)(2,1)S(1)}, bf16[2,48,128]{2,1,0:T(8,128)(2,1)S(1)}, u32[]{:S(2)}, u32[]{:S(2)}) collective-permute-start(bf16[2,48,128]{2,1,0:T(8,128)(2,1)S(1)} %dynamic-slice_bitcast_fusion.22), channel_id=1, source_target_pairs={{0,4},{1,5},{2,6},{3,7},{4,0},{5,1},{6,2},{7,3},{8,12},{9,13},{10,... | collective-permute-start | bytes 73736 | tf_op jit(solution)/shard_map/ppermute | solution.py:385
  309.7 4.7 %collective-permute-start.62 = (bf16[48,128]{1,0:T(8,128)(2,1)S(1)}, bf16[48,128]{1,0:T(8,128)(2,1)S(1)}, u32[]{:S(2)}, u32[]{:S(2)}) collective-permute-start(bf16[48,128]{1,0:T(8,128)(2,1)S(1)} %fusion.83), channel_id=1, source_target_pairs={{0,8},{1,9},{2,10},{3,11},{4,12},{5,13},{6,14},{7,15},{8,0},{9,1},... | collective-permute-start | bytes 36872 | tf_op jit(solution)/shard_map/ppermute | solution.py:385
  311.2 41.7 %collective-permute-start.42 = (bf16[16,96,768]{2,1,0:T(8,128)(2,1)}, bf16[16,96,768]{2,1,0:T(8,128)(2,1)}, u32[]{:S(2)}, u32[]{:S(2)}) collective-permute-start(bf16[16,96,768]{2,1,0:T(8,128)(2,1)} %dynamic-slice_bitcast_fusion.1), channel_id=1, source_target_pairs={{0,16},{16,0},{1,17},{17,1},{2,18},{18,2},{3,19},{19,3},{4,20},{20... | collective-permute-start | bytes 7077896 | tf_op jit(solution)/shard_map/ppermute | solution.py:385
  311.3 5.4 %collective-permute-start.57 = (bf16[48,128]{1,0:T(8,128)(2,1)S(1)}, bf16[48,128]{1,0:T(8,128)(2,1)S(1)}, u32[]{:S(2)}, u32[]{:S(2)}) collective-permute-start(bf16[48,128]{1,0:T(8,128)(2,1)S(1)} %fusion.81), channel_id=1, source_target_pairs={{0,8},{1,9},{2,10},{3,11},{4,12},{5,13},{6,14},{7,15},{8,0},{9,1},... | collective-permute-start | bytes 36872 | tf_op jit(solution)/shard_map/ppermute | solution.py:385
  314.4 6.6 %collective-permute-start.34 = (f32[24,1536]{1,0:T(8,128)S(1)}, f32[24,1536]{1,0:T(8,128)}, u32[]{:S(2)}, u32[]{:S(2)}) collective-permute-start(f32[24,1536]{1,0:T(8,128)S(1)} %add.561), channel_id=1, source_target_pairs={{0,2},{1,3},{2,0},{3,1},{4,6},{5,7},{6,4},{7,5},{8,10},{9,11},{10,... | collective-permute-start | bytes 442376 | tf_op jit(solution)/shard_map/ppermute | solution.py:385
  318.5 16.0 %collective-permute-start.70 = (bf16[2,2,2,48,768]{4,3,0,1,2:T(8,128)(2,1)}, bf16[2,2,2,48,768]{4,3,0,1,2:T(8,128)(2,1)}, u32[]{:S(2)}, u32[]{:S(2)}) collective-permute-start(bf16[2,2,2,48,768]{4,3,0,1,2:T(8,128)(2,1)} %bitcast.371), channel_id=1, source_target_pairs={{0,1},{1,0},{2,3},{3,2},{4,5},{5,4},{6,7},{7,6},{8,9},{9,8},{10,11... | collective-permute-start | bytes 1769480 | tf_op jit(solution)/shard_map/ppermute | solution.py:385
  321.9 5.6 %collective-permute-start.35 = (f32[24,1536]{1,0:T(8,128)S(1)}, f32[24,1536]{1,0:T(8,128)}, u32[]{:S(2)}, u32[]{:S(2)}) collective-permute-start(f32[24,1536]{1,0:T(8,128)S(1)} %add.562), channel_id=1, source_target_pairs={{0,4},{1,5},{2,6},{3,7},{4,0},{5,1},{6,2},{7,3},{8,12},{9,13},{10,... | collective-permute-start | bytes 442376 | tf_op jit(solution)/shard_map/ppermute | solution.py:385
  327.6 12.2 %collective-permute-start.41 = (f32[24,1536]{1,0:T(8,128)S(1)}, f32[24,1536]{1,0:T(8,128)S(1)}, u32[]{:S(2)}, u32[]{:S(2)}) collective-permute-start(f32[24,1536]{1,0:T(8,128)S(1)} %add.568), channel_id=1, source_target_pairs={{0,8},{1,9},{2,10},{3,11},{4,12},{5,13},{6,14},{7,15},{8,0},{9,1},... | collective-permute-start | bytes 442376 | tf_op jit(solution)/shard_map/ppermute | solution.py:385
  329.2 12.9 %collective-permute-start.36 = (f32[24,1536]{1,0:T(8,128)S(1)}, f32[24,1536]{1,0:T(8,128)S(1)}, u32[]{:S(2)}, u32[]{:S(2)}) collective-permute-start(f32[24,1536]{1,0:T(8,128)S(1)} %add.563), channel_id=1, source_target_pairs={{0,8},{1,9},{2,10},{3,11},{4,12},{5,13},{6,14},{7,15},{8,0},{9,1},... | collective-permute-start | bytes 442376 | tf_op jit(solution)/shard_map/ppermute | solution.py:385
  334.6 14.9 %collective-permute-start.65 = (bf16[2,2,2,48,768]{4,3,0,1,2:T(8,128)(2,1)S(1)}, bf16[2,2,2,48,768]{4,3,0,1,2:T(8,128)(2,1)S(1)}, u32[]{:S(2)}, u32[]{:S(2)}) collective-permute-start(bf16[2,2,2,48,768]{4,3,0,1,2:T(8,128)(2,1)S(1)} %bitcast.443), channel_id=1, source_target_pairs={{0,1},{1,0},{2,3},{3,2},{4,5},{5,4},{6,7},{7,6},{8,9},{9,8},{10,11... | collective-permute-start | bytes 1769480 | tf_op jit(solution)/shard_map/ppermute | solution.py:385
  339.8 7.8 %collective-permute-start.71 = (bf16[2,2,48,768]{3,2,0,1:T(8,128)(2,1)S(1)}, bf16[2,2,48,768]{3,2,0,1:T(8,128)(2,1)S(1)}, u32[]{:S(2)}, u32[]{:S(2)}) collective-permute-start(bf16[2,2,48,768]{3,2,0,1:T(8,128)(2,1)S(1)} %dynamic-slice_bitcast_fusion.6), channel_id=1, source_target_pairs={{0,2},{1,3},{2,0},{3,1},{4,6},{5,7},{6,4},{7,5},{8,10},{9,11},{10,... | collective-permute-start | bytes 884744 | tf_op jit(solution)/shard_map/ppermute | solution.py:385
  347.7 10.5 %collective-permute-start.72 = (bf16[2,48,768]{2,1,0:T(8,128)(2,1)S(1)}, bf16[2,48,768]{2,1,0:T(8,128)(2,1)S(1)}, u32[]{:S(2)}, u32[]{:S(2)}) collective-permute-start(bf16[2,48,768]{2,1,0:T(8,128)(2,1)S(1)} %dynamic-slice_bitcast_fusion.12), channel_id=1, source_target_pairs={{0,4},{1,5},{2,6},{3,7},{4,0},{5,1},{6,2},{7,3},{8,12},{9,13},{10,... | collective-permute-start | bytes 442376 | tf_op jit(solution)/shard_map/ppermute | solution.py:385
  352.5 29.0 %collective-permute-start.48 = (bf16[2,2,2,96,768]{4,3,0,1,2:T(8,128)(2,1)S(1)}, bf16[2,2,2,96,768]{4,3,0,1,2:T(8,128)(2,1)S(1)}, u32[]{:S(2)}, u32[]{:S(2)}) collective-permute-start(bf16[2,2,2,96,768]{4,3,0,1,2:T(8,128)(2,1)S(1)} %bitcast.430), channel_id=1, source_target_pairs={{0,1},{1,0},{2,3},{3,2},{4,5},{5,4},{6,7},{7,6},{8,9},{9,8},{10,11... | collective-permute-start | bytes 3538952 | tf_op jit(solution)/shard_map/ppermute | solution.py:385
  355.5 49.0 %collective-permute-start.43 = (bf16[2,2,2,96,768]{4,3,0,1,2:T(8,128)(2,1)S(1)}, bf16[2,2,2,96,768]{4,3,0,1,2:T(8,128)(2,1)S(1)}, u32[]{:S(2)}, u32[]{:S(2)}) collective-permute-start(bf16[2,2,2,96,768]{4,3,0,1,2:T(8,128)(2,1)S(1)} %bitcast.431), channel_id=1, source_target_pairs={{0,1},{1,0},{2,3},{3,2},{4,5},{5,4},{6,7},{7,6},{8,9},{9,8},{10,11... | collective-permute-start | bytes 3538952 | tf_op jit(solution)/shard_map/ppermute | solution.py:385
  357.3 7.2 %collective-permute-start.66 = (bf16[2,2,48,768]{3,2,0,1:T(8,128)(2,1)S(1)}, bf16[2,2,48,768]{3,2,0,1:T(8,128)(2,1)S(1)}, u32[]{:S(2)}, u32[]{:S(2)}) collective-permute-start(bf16[2,2,48,768]{3,2,0,1:T(8,128)(2,1)S(1)} %dynamic-slice_bitcast_fusion.7), channel_id=1, source_target_pairs={{0,2},{1,3},{2,0},{3,1},{4,6},{5,7},{6,4},{7,5},{8,10},{9,11},{10,... | collective-permute-start | bytes 884744 | tf_op jit(solution)/shard_map/ppermute | solution.py:385
  358.3 69.4 %collective-permute-start.73 = (bf16[48,768]{1,0:T(8,128)(2,1)S(1)}, bf16[48,768]{1,0:T(8,128)(2,1)S(1)}, u32[]{:S(2)}, u32[]{:S(2)}) collective-permute-start(bf16[48,768]{1,0:T(8,128)(2,1)S(1)} %dynamic-slice_bitcast_fusion.17), channel_id=1, source_target_pairs={{0,8},{1,9},{2,10},{3,11},{4,12},{5,13},{6,14},{7,15},{8,0},{9,1},... | collective-permute-start | bytes 221192 | tf_op jit(solution)/shard_map/ppermute | solution.py:385
  364.6 41.2 %collective-permute-start.67 = (bf16[2,48,768]{2,1,0:T(8,128)(2,1)S(1)}, bf16[2,48,768]{2,1,0:T(8,128)(2,1)S(1)}, u32[]{:S(2)}, u32[]{:S(2)}) collective-permute-start(bf16[2,48,768]{2,1,0:T(8,128)(2,1)S(1)} %dynamic-slice_bitcast_fusion.13), channel_id=1, source_target_pairs={{0,4},{1,5},{2,6},{3,7},{4,0},{5,1},{6,2},{7,3},{8,12},{9,13},{10,... | collective-permute-start | bytes 442376 | tf_op jit(solution)/shard_map/ppermute | solution.py:385
  381.8 26.2 %collective-permute-start.49 = (bf16[2,2,96,768]{3,2,0,1:T(8,128)(2,1)S(1)}, bf16[2,2,96,768]{3,2,0,1:T(8,128)(2,1)S(1)}, u32[]{:S(2)}, u32[]{:S(2)}) collective-permute-start(bf16[2,2,96,768]{3,2,0,1:T(8,128)(2,1)S(1)} %dynamic-slice_bitcast_fusion.4), channel_id=1, source_target_pairs={{0,2},{1,3},{2,0},{3,1},{4,6},{5,7},{6,4},{7,5},{8,10},{9,11},{10,... | collective-permute-start | bytes 1769480 | tf_op jit(solution)/shard_map/ppermute | solution.py:385
  404.9 13.2 %collective-permute-start.44 = (bf16[2,2,96,768]{3,2,0,1:T(8,128)(2,1)S(1)}, bf16[2,2,96,768]{3,2,0,1:T(8,128)(2,1)S(1)}, u32[]{:S(2)}, u32[]{:S(2)}) collective-permute-start(bf16[2,2,96,768]{3,2,0,1:T(8,128)(2,1)S(1)} %dynamic-slice_bitcast_fusion.5), channel_id=1, source_target_pairs={{0,2},{1,3},{2,0},{3,1},{4,6},{5,7},{6,4},{7,5},{8,10},{9,11},{10,... | collective-permute-start | bytes 1769480 | tf_op jit(solution)/shard_map/ppermute | solution.py:385
  405.9 21.8 %collective-permute-start.68 = (bf16[48,768]{1,0:T(8,128)(2,1)S(1)}, bf16[48,768]{1,0:T(8,128)(2,1)S(1)}, u32[]{:S(2)}, u32[]{:S(2)}) collective-permute-start(bf16[48,768]{1,0:T(8,128)(2,1)S(1)} %dynamic-slice_bitcast_fusion.18), channel_id=1, source_target_pairs={{0,8},{1,9},{2,10},{3,11},{4,12},{5,13},{6,14},{7,15},{8,0},{9,1},... | collective-permute-start | bytes 221192 | tf_op jit(solution)/shard_map/ppermute | solution.py:385
  408.2 11.1 %collective-permute-start.50 = (bf16[2,96,768]{2,1,0:T(8,128)(2,1)S(1)}, bf16[2,96,768]{2,1,0:T(8,128)(2,1)S(1)}, u32[]{:S(2)}, u32[]{:S(2)}) collective-permute-start(bf16[2,96,768]{2,1,0:T(8,128)(2,1)S(1)} %dynamic-slice_bitcast_fusion.8), channel_id=1, source_target_pairs={{0,4},{1,5},{2,6},{3,7},{4,0},{5,1},{6,2},{7,3},{8,12},{9,13},{10,... | collective-permute-start | bytes 884744 | tf_op jit(solution)/shard_map/ppermute | solution.py:385
  418.2 9.1 %collective-permute-start.45 = (bf16[2,96,768]{2,1,0:T(8,128)(2,1)S(1)}, bf16[2,96,768]{2,1,0:T(8,128)(2,1)S(1)}, u32[]{:S(2)}, u32[]{:S(2)}) collective-permute-start(bf16[2,96,768]{2,1,0:T(8,128)(2,1)S(1)} %dynamic-slice_bitcast_fusion.9), channel_id=1, source_target_pairs={{0,4},{1,5},{2,6},{3,7},{4,0},{5,1},{6,2},{7,3},{8,12},{9,13},{10,... | collective-permute-start | bytes 884744 | tf_op jit(solution)/shard_map/ppermute | solution.py:385
  419.5 8.4 %collective-permute-start.51 = (bf16[96,768]{1,0:T(8,128)(2,1)S(1)}, bf16[96,768]{1,0:T(8,128)(2,1)S(1)}, u32[]{:S(2)}, u32[]{:S(2)}) collective-permute-start(bf16[96,768]{1,0:T(8,128)(2,1)S(1)} %dynamic-slice_bitcast_fusion.14), channel_id=1, source_target_pairs={{0,8},{1,9},{2,10},{3,11},{4,12},{5,13},{6,14},{7,15},{8,0},{9,1},... | collective-permute-start | bytes 442376 | tf_op jit(solution)/shard_map/ppermute | solution.py:385
  427.5 7.1 %collective-permute-start.46 = (bf16[96,768]{1,0:T(8,128)(2,1)S(1)}, bf16[96,768]{1,0:T(8,128)(2,1)S(1)}, u32[]{:S(2)}, u32[]{:S(2)}) collective-permute-start(bf16[96,768]{1,0:T(8,128)(2,1)S(1)} %dynamic-slice_bitcast_fusion.15), channel_id=1, source_target_pairs={{0,8},{1,9},{2,10},{3,11},{4,12},{5,13},{6,14},{7,15},{8,0},{9,1},... | collective-permute-start | bytes 442376 | tf_op jit(solution)/shard_map/ppermute | solution.py:385
  427.8 8.2 %collective-permute-start.74 = (f32[48,768]{1,0:T(8,128)S(1)}, f32[48,768]{1,0:T(8,128)S(1)}, u32[]{:S(2)}, u32[]{:S(2)}) collective-permute-start(f32[48,768]{1,0:T(8,128)S(1)} %get-tuple-element.173), channel_id=1, source_target_pairs={{0,16},{16,0},{1,17},{17,1},{2,18},{18,2},{3,19},{19,3},{4,20},{20... | collective-permute-start | bytes 442376 | tf_op jit(solution)/shard_map/ppermute | solution.py:385
  (67 other events, 717.2 us)
